TPU v7x, 128 devices: a whole 4x4x4 slice. The times are simulated.
128 devices in a mesh: pb: 8 (over x, y_lo), pa: 16 (over z, y_hi, core).
Axes of the slice: x: 4, y: 4 (y_hi: 2, y_lo: 2; y = y_hi * 2 + y_lo), z: 4, core: 2. Of those that a mesh axis runs over, the one named last changes fastest.
Arguments:
- query_cache: bfloat16 [8, 512, 4096], P('pb', 'pa'), may hold values from -0.4 to 0.4
- passage_cache: bfloat16 [16, 256, 4096], P('pa', 'pb'), may hold values from -0.4 to 0.4
- positive: int32 [8, 512], P('pb', 'pa'), may hold values from 0 to 4095
- query_tokens: bfloat16 [8, 16, 128, 4096], P('pb', 'pa'), may hold values from -6 to 6
- passage_tokens: bfloat16 [16, 8, 768, 4096], P('pa', 'pb'), may hold values from -6 to 6
- query_lengths: int32 [8, 16, 4], P('pb', 'pa'), may hold values from 1 to 64, 128 in all within a row
- passage_lengths: int32 [16, 8, 2], P('pa', 'pb'), may hold values from 1 to 512, 768 in all within a row
- norm_gain: bfloat16 [4096], P(('pb', 'pa')), may hold values from 0.099609375 to 1.8984375
- adapter_down: bfloat16 [4096, 512], P(('pb', 'pa')), may hold values from -0.09375 to 0.09375
- adapter_up: bfloat16 [512, 4096], P(('pb', 'pa')), may hold values from -0.25 to 0.25
Outputs:
- query_grad: bfloat16 [8, 512, 4096], P('pb', 'pa')
- passage_grad: bfloat16 [16, 256, 4096], P('pa', 'pb')
- down_grad: float32 [4096, 512], P(('pb', 'pa'))
- up_grad: float32 [512, 4096], P(('pb', 'pa'))
- gain_grad: float32 [4096], P(('pb', 'pa'))
All inputs are finite; a program needn't handle non-finite values.
Results may differ from a plain program's by a relative error of at most 0.028.
Values may be sent and summed in bfloat16 or wider, within the bound.
No kernel may reach another device: no remote copies, remote signals or barrier semaphores. Data moves between devices by JAX's collectives and lax.ppermute only.
A program may use at most 128 MiB of HBM per device.

v0:
```python
import jax
import jax.numpy as jnp
from jax import lax
from jax.experimental import pallas as pl
from jax.experimental.pallas import tpu as pltpu
from jax.sharding import Mesh, PartitionSpec as P

scale = 1.0 / 0.05
epsilon = 1e-06
bf16 = jnp.bfloat16
f32 = jnp.float32
everyone = ("x", "yl", "z", "yh", "c")
swap2 = [(0, 1), (1, 0)]
barrier = lax.optimization_barrier


def shift(value, axis, step, size):
    return lax.ppermute(value, axis, [(i, (i + step) % size) for i in range(size)])


def swap(value, axis):
    return lax.ppermute(value, axis, swap2)


def ring_sides(block, ring):
    return shift(block, ring, 1, 4), shift(block, ring, 3, 4)


def ring_far(before, after, ring):
    half = before.shape[0] // 2
    return shift(before[:half], ring, 1, 4), shift(after[half:], ring, 3, 4)


def ring_sum(parts, ring, size):
    return [parts[0]] + [shift(parts[k], ring, size - k, size) for k in range(1, size)]


def cut_rows(part, count):
    rows = part.shape[0] // count
    return [part[k * rows : (k + 1) * rows] for k in range(count)]


def add_up(terms):
    total = terms[0].astype(f32)
    for t in terms[1:]:
        total = total + t.astype(f32)
    return total


def pair_sum(total, pair):
    half = total.shape[0] // 2
    return (total[:half] + swap(total[half:].astype(bf16), pair).astype(f32)).astype(bf16)


gelu_root = 0.7978845608028654
gelu_cube = 0.044715
kernel_room = pltpu.CompilerParams(vmem_limit_bytes=60 * 1024 * 1024)
light = pl.CostEstimate(flops=0, bytes_accessed=0, transcendentals=0)
any_space = pl.BlockSpec(memory_space=pl.ANY)
in_vmem = pl.BlockSpec(memory_space=pltpu.VMEM)
in_smem = pl.BlockSpec(memory_space=pltpu.SMEM)


turned = (((0,), (0,)), ((), ()))
contract = (((1,), (1,)), ((), ()))


def load_blocks(parts, wholes, sems):
    copies, n = [], 0
    for blocks, whole in zip(parts, wholes):
        row = 0
        for block in blocks:
            copies.append(pltpu.make_async_copy(block, whole.at[pl.ds(row, block.shape[0])], sems.at[n]))
            row, n = row + block.shape[0], n + 1
    for c in copies:
        c.start()
    return copies


def wait_all(copies):
    for c in copies:
        c.wait()


def score_kernel(n_q, n_p, *refs):
    q_blocks, p_blocks = refs[:n_q], refs[n_q : n_q + n_p]
    scores, top, total, q_all, p_all, sems = refs[n_q + n_p :]
    wait_all(load_blocks((q_blocks, p_blocks), (q_all, p_all), sems))
    s = lax.dot_general(q_all[...], p_all[...], contract, preferred_element_type=f32) * scale
    scores[...] = s
    m = jnp.max(s, axis=1, keepdims=True)
    top[...] = m
    total[...] = jnp.sum(jnp.exp(s - m), axis=1, keepdims=True)


def rows_of(blocks):
    return sum(b.shape[0] for b in blocks)


def block_scratch(q_blocks, p_blocks):
    width = q_blocks[0].shape[1]
    return [
        pltpu.VMEM((rows_of(q_blocks), width), bf16),
        pltpu.VMEM((rows_of(p_blocks), width), bf16),
        pltpu.SemaphoreType.DMA((len(q_blocks) + len(p_blocks),)),
    ]


def score_block(q_blocks, p_blocks):
    n_q, n_p = rows_of(q_blocks), rows_of(p_blocks)
    column = jax.ShapeDtypeStruct((n_q, 1), f32)
    return pl.pallas_call(
        lambda *refs: score_kernel(len(q_blocks), len(p_blocks), *refs),
        out_shape=(jax.ShapeDtypeStruct((n_q, n_p), f32), column, column),
        in_specs=[any_space] * (len(q_blocks) + len(p_blocks)),
        out_specs=(in_vmem,) * 3,
        scratch_shapes=block_scratch(q_blocks, p_blocks),
        compiler_params=kernel_room,
        cost_estimate=light,
    )(*q_blocks, *p_blocks)


def couple_kernel(n_q, n_p, sizes, counts, spot, scores, stat, columns, *refs):
    q_blocks, p_blocks = refs[:n_q], refs[n_q : n_q + n_p]
    coupling, q_few, p_few, q_all, p_all, sems = refs[n_q + n_p :]
    copies = load_blocks((q_blocks, p_blocks), (q_all, p_all), sems)
    soft = jnp.exp(scores[...] - stat[:, 0:1]) / stat[:, 1:2]
    hit = (stat[:, 2:3].astype(jnp.int32) == columns[...]).astype(f32)
    link = (soft - hit).astype(bf16)
    coupling[...] = link
    wait_all(copies)
    rows, cols = link.shape
    nx, nyl, nz, nyh, nc = sizes
    yl, yh, core, x, z = (spot[k] for k in range(head))
    q_seqs, q_row, p_seqs, p_row = counts
    n_q_owners = q_few.shape[0]

    n_few = n_q_owners * q_seqs
    few_i = lax.broadcasted_iota(jnp.int32, (n_few, rows), 0)
    here = lax.broadcasted_iota(jnp.int32, (n_few, rows), 1)
    seq, owner = few_i % q_seqs, few_i // q_seqs
    step = (z - owner // nyh + nz) % nz * nyh + (yh - owner % nyh + nyh) % nyh
    pick = (here == step * q_row + seq).astype(bf16)
    first = jnp.dot(pick, link, preferred_element_type=f32).astype(bf16)
    found = jnp.dot(first, p_all[...], preferred_element_type=f32) * scale
    for k in range(n_q_owners):
        q_few[k] = found[k * q_seqs : (k + 1) * q_seqs].astype(bf16)

    n_few = p_few.shape[0] * p_seqs
    few_i = lax.broadcasted_iota(jnp.int32, (n_few, cols), 0)
    here = lax.broadcasted_iota(jnp.int32, (n_few, cols), 1)
    seq, owner = few_i % p_seqs, few_i // p_seqs
    x_step = (x - owner // (nyl * nc) + nx) % nx
    yl_step = (yl - owner // nc % nyl + nyl) % nyl
    core_step = (core - owner % nc + nc) % nc
    pick = (here == ((core_step * nx + x_step) * nyl + yl_step) * p_row + seq).astype(bf16)
    first = lax.dot_general(pick, link, contract, preferred_element_type=f32).astype(bf16)
    found = jnp.dot(first, q_all[...], preferred_element_type=f32) * scale
    for k in range(p_few.shape[0]):
        p_few[k] = found[k * p_seqs : (k + 1) * p_seqs].astype(bf16)


def couple(spot, scores, stat, columns, q_blocks, p_blocks, sizes, counts):
    n_q, n_p = scores.shape
    width = q_blocks[0].shape[1]
    q_seqs, q_row, p_seqs, p_row = counts
    return pl.pallas_call(
        lambda *refs: couple_kernel(len(q_blocks), len(p_blocks), sizes, counts, *refs),
        out_shape=(
            jax.ShapeDtypeStruct((n_q, n_p), bf16),
            jax.ShapeDtypeStruct((n_q // q_row, q_seqs, width), bf16),
            jax.ShapeDtypeStruct((n_p // p_row, p_seqs, width), bf16),
        ),
        in_specs=[in_smem] + [in_vmem] * 3 + [any_space] * (len(q_blocks) + len(p_blocks)),
        out_specs=[in_vmem] * 3,
        scratch_shapes=block_scratch(q_blocks, p_blocks),
        compiler_params=kernel_room,
        cost_estimate=light,
    )(spot, scores, stat, columns, *q_blocks, *p_blocks)


def ring_add_kernel(n, *refs):
    total = refs[0][...].astype(f32)
    for r in refs[1:n]:
        total = total + r[...].astype(f32)
    half = total.shape[0] // 2
    refs[n][...] = total[:half]
    refs[n + 1][...] = total[half:].astype(bf16)


def ring_add(terms):
    rows, width = terms[0].shape
    tile = width // 2

    def cut(n):
        return pl.BlockSpec((n, tile), lambda i: (0, i))

    return pl.pallas_call(
        lambda *refs: ring_add_kernel(len(terms), *refs),
        grid=(2,),
        out_shape=(jax.ShapeDtypeStruct((rows // 2, width), f32), jax.ShapeDtypeStruct((rows // 2, width), bf16)),
        in_specs=[cut(rows)] * len(terms),
        out_specs=(cut(rows // 2),) * 2,
        compiler_params=kernel_room,
        cost_estimate=pl.CostEstimate(
            flops=0, bytes_accessed=2 * rows * width * (len(terms) + 2), transcendentals=0
        ),
    )(*terms)


def core_add_kernel(n, *refs):
    for keep, came, out in zip(refs[:n], refs[n : 2 * n], refs[2 * n :]):
        out[...] = (keep[...].astype(f32) + came[...].astype(f32)).astype(bf16)


def core_add(keep, came):
    steps = 2
    width = keep[0].shape[-1]

    def cut(a):
        return pl.BlockSpec(a.shape[:-1] + (width // steps,), lambda i: (0,) * (a.ndim - 1) + (i,))

    return pl.pallas_call(
        lambda *refs: core_add_kernel(len(keep), *refs),
        grid=(steps,),
        out_shape=[jax.ShapeDtypeStruct(a.shape, bf16) for a in keep],
        in_specs=[cut(a) for a in (*keep, *came)],
        out_specs=[cut(a) for a in keep],
        compiler_params=kernel_room,
        cost_estimate=light,
    )(*keep, *came)


def chip_add_kernel(n, keep, *refs):
    out = refs[n]
    rows = refs[0].shape[0]
    for k in range(n):
        here = pl.ds(k * rows, rows)
        out[here] = (keep[here].astype(f32) + refs[k][...].astype(f32)).astype(bf16)


def chip_add(keep, came):
    steps = 2
    width = keep.shape[-1]

    def cut(a):
        return pl.BlockSpec(a.shape[:-1] + (width // steps,), lambda i: (0,) * (a.ndim - 1) + (i,))

    return pl.pallas_call(
        lambda *refs: chip_add_kernel(len(came), *refs),
        grid=(steps,),
        out_shape=jax.ShapeDtypeStruct(keep.shape, bf16),
        in_specs=[cut(keep)] + [cut(a) for a in came],
        out_specs=cut(keep),
        compiler_params=kernel_room,
        cost_estimate=light,
    )(keep, *came)


def parts_kernel(n_blocks, n_out, turn, coupling, *refs):
    blocks, outs = refs[:n_blocks], refs[n_blocks : n_blocks + n_out]
    link = coupling[...]
    rows = outs[0].shape[0]
    whole = jnp.concatenate([b[...] for b in blocks], axis=0)
    if turn:
        part = lax.dot_general(link, whole, turned, preferred_element_type=f32)
    else:
        part = jnp.dot(link, whole, preferred_element_type=f32)
    part = (part * scale).astype(bf16)
    for k in range(n_out):
        outs[k][...] = part[k * rows : (k + 1) * rows]


def grad_parts(coupling, blocks, n_out, turn):
    n_q, n_p = coupling.shape
    width = blocks[0].shape[1]
    tile = 2048
    rows = (n_p if turn else n_q) // n_out

    def cut(n):
        return pl.BlockSpec((n, tile), lambda i: (0, i))

    return pl.pallas_call(
        lambda *refs: parts_kernel(len(blocks), n_out, turn, *refs),
        grid=(width // tile,),
        out_shape=[jax.ShapeDtypeStruct((rows, width), bf16)] * n_out,
        in_specs=[pl.BlockSpec((n_q, n_p), lambda i: (0, 0))] + [cut(b.shape[0]) for b in blocks],
        out_specs=[cut(rows)] * n_out,
        compiler_params=kernel_room,
        cost_estimate=pl.CostEstimate(
            flops=2 * n_q * n_p * width, bytes_accessed=2 * (n_q + n_p) * width, transcendentals=0
        ),
    )(coupling, *blocks)


def down_kernel(core, tok_q, tok_p, inner_q, inner_p, keep, *gives):
    part = lax.dot_general(tok_p[...], inner_p[...], turned, preferred_element_type=f32)
    part = part + lax.dot_general(tok_q[...], inner_q[...], turned, preferred_element_type=f32)
    chips, rows, hidden = keep.shape
    part = part.astype(bf16).reshape(chips, 2, rows, hidden)
    first = core[2] == 0
    piece = pl.program_id(0) // (pl.num_programs(0) // len(gives))

    @pl.when(first)
    def _():
        keep[...] = part[:, 0]

    @pl.when(jnp.logical_not(first))
    def _():
        keep[...] = part[:, 1]

    for k, give in enumerate(gives):

        @pl.when((piece == k) & first)
        def _():
            give[...] = part[:, 1]

        @pl.when((piece == k) & jnp.logical_not(first))
        def _():
            give[...] = part[:, 0]


def down_parts(spot, tok_q, tok_p, inner_q, inner_p, rows):
    width, hidden = tok_q.shape[1], inner_q.shape[1]
    tile, pieces = 1024, 4
    chips = tile // (2 * rows)
    steps = width // tile
    each = steps // pieces
    n_chips = width // (2 * rows)

    def cut(a):
        return pl.BlockSpec((a.shape[0], tile), lambda i: (0, i))

    def piece_spec(k):
        return pl.BlockSpec((chips, rows, hidden), lambda i: (jnp.clip(i - k * each, 0, each - 1), 0, 0))

    out = pl.pallas_call(
        down_kernel,
        grid=(steps,),
        out_shape=[jax.ShapeDtypeStruct((n_chips, rows, hidden), bf16)]
        + [jax.ShapeDtypeStruct((n_chips // pieces, rows, hidden), bf16)] * pieces,
        in_specs=[
            in_smem, cut(tok_q), cut(tok_p),
            pl.BlockSpec(inner_q.shape, lambda i: (0, 0)), pl.BlockSpec(inner_p.shape, lambda i: (0, 0)),
        ],
        out_specs=[pl.BlockSpec((chips, rows, hidden), lambda i: (i, 0, 0))] + [piece_spec(k) for k in range(pieces)],
        compiler_params=kernel_room,
        cost_estimate=pl.CostEstimate(
            flops=2 * (tok_q.shape[0] + tok_p.shape[0]) * width * hidden, bytes_accessed=4 * width * hidden,
            transcendentals=0,
        ),
    )(spot, tok_q, tok_p, inner_q, inner_p)
    return out[0], out[1:]


ring_places = ((0, 0, 2), (1, 0, 2), (2, 0, 1), (2, 1, 1), (3, 0, 2))
head = 5


def token_kernel(n_seq, n_blocks, spot, *rest):
    blocks = rest[:n_blocks]
    tok_q, tok_p, slope_q, slope_p, sums, weights, sems = rest[n_blocks:]
    i = pl.program_id(0)

    @pl.when(i == 0)
    def _():
        copies = []
        for k in range(n_blocks):
            step, first, count = ring_places[k % len(ring_places)]
            x = lax.rem(spot[3] - step + 4, 4)
            core = lax.rem(spot[2] + k // len(ring_places), 2)
            copies.append(
                pltpu.make_async_copy(
                    blocks[k].at[:, :, :, pl.ds(0, weights.shape[5])],
                    weights.at[x, pl.ds(first, count), :, :, core],
                    sems.at[k],
                )
            )
        for c in copies:
            c.start()
        sums[...] = jnp.zeros_like(sums)
        for c in copies:
            c.wait()

    hidden = weights.shape[-1]

    def work(tok, slope, first_row):
        rows = tok.shape[0]
        wide = tok[...].astype(f32)
        inverse = lax.rsqrt(jnp.mean(wide * wide, axis=1, keepdims=True) + epsilon)
        pre = jnp.dot(tok[...], weights[...].reshape(-1, hidden), preferred_element_type=f32) * inverse
        square = pre * pre
        bend = jnp.tanh(gelu_root * pre * (1.0 + gelu_cube * square))
        up = 0.5 * (1.0 + bend)
        active = (pre * up).astype(bf16)
        steep = up + 0.5 * pre * (1.0 - bend * bend) * (gelu_root * (1.0 + 3.0 * gelu_cube * square))
        slope[...] = steep * inverse
        seq = lax.broadcasted_iota(jnp.int32, (sums.shape[0], rows), 0)
        row = lax.broadcasted_iota(jnp.int32, (sums.shape[0], rows), 1) + first_row
        member = jnp.zeros((sums.shape[0], rows), f32)
        for k in range(n_seq):
            inside = (row >= spot[head + k]) & (row < spot[head + n_seq + k]) & (seq == k)
            member = jnp.where(inside, 1.0, member)
        sums[...] += jnp.dot(member.astype(bf16), active, preferred_element_type=f32)

    @pl.when(i == 0)
    def _():
        work(tok_q, slope_q, 0)

    @pl.when(i > 0)
    def _():
        work(tok_p, slope_p, tok_q.shape[0] + (i - 1) * tok_p.shape[0])


def token_half(spot, blocks, tok_q, tok_p, n_seq, n_seq8):
    width = tok_q.shape[1]
    nyl, nz, nyh, both, hidden = blocks[0].shape
    d_own = width // (4 * nyl * nz * nyh * 2)
    steps = 2
    tile = tok_p.shape[0] // steps

    def tile_of(i):
        return (jnp.maximum(i - 1, 0), 0)

    return pl.pallas_call(
        lambda *refs: token_kernel(n_seq, len(blocks), *refs),
        grid=(steps + 1,),
        out_shape=(
            jax.ShapeDtypeStruct((tok_q.shape[0], hidden), f32),
            jax.ShapeDtypeStruct((tok_p.shape[0], hidden), f32),
            jax.ShapeDtypeStruct((n_seq8, hidden), f32),
        ),
        in_specs=[in_smem] + [any_space] * len(blocks)
        + [pl.BlockSpec(tok_q.shape, lambda i: (0, 0)), pl.BlockSpec((tile, width), tile_of)],
        out_specs=(
            pl.BlockSpec((tok_q.shape[0], hidden), lambda i: (0, 0)),
            pl.BlockSpec((tile, hidden), tile_of),
            pl.BlockSpec((n_seq8, hidden), lambda i: (0, 0)),
        ),
        scratch_shapes=[
            pltpu.VMEM((4, nyl, nz, nyh, 2, d_own, hidden), bf16), pltpu.SemaphoreType.DMA((len(blocks),))
        ],
        compiler_params=kernel_room,
        cost_estimate=light,
    )(spot, *blocks, tok_q, tok_p)


def hidden_kernel(n_blocks, units, grads, *refs):
    blocks = refs[:n_blocks]
    out, lines, sems = refs[n_blocks:]
    rows, line = lines.shape[-2:]
    copies = [
        pltpu.make_async_copy(
            blocks[k].at[:, :, :, pl.ds(blocks[k].shape[3] - rows, rows)],
            lines.at[step, pl.ds(first, count)],
            sems.at[k],
        )
        for k, (step, first, count) in enumerate(ring_places)
    ]
    for c in copies:
        c.start()
    n_seq, width = grads.shape
    per_unit = width // line
    cut = jnp.concatenate([grads[:, j * line : (j + 1) * line] for j in range(per_unit)], axis=0)
    for c in copies:
        c.wait()
    flat = lines[...].reshape(-1, line)
    found = lax.dot_general(cut, flat, contract, preferred_element_type=f32)
    which = lax.broadcasted_iota(jnp.int32, (n_seq, flat.shape[0]), 1) % per_unit
    kept = jnp.zeros((n_seq, flat.shape[0]), f32)
    for j in range(per_unit):
        kept = jnp.where(which == j, found[j * n_seq : (j + 1) * n_seq], kept)
    source = lax.broadcasted_iota(jnp.int32, (flat.shape[0], units), 0) // per_unit
    to = lax.broadcasted_iota(jnp.int32, (flat.shape[0], units), 1)
    gather = (source == to).astype(bf16)
    total = jnp.zeros((n_seq, units), f32)
    for _ in range(3):
        piece = kept.astype(bf16)
        total = total + jnp.dot(piece, gather, preferred_element_type=f32)
        kept = kept - piece.astype(f32)
    out[...] = total


def hidden_of(grads, blocks, rows, units):
    shape = blocks[0].shape
    return pl.pallas_call(
        lambda *refs: hidden_kernel(len(blocks), units, *refs),
        out_shape=jax.ShapeDtypeStruct((grads.shape[0], units), f32),
        in_specs=[in_vmem] + [any_space] * len(blocks),
        out_specs=in_vmem,
        scratch_shapes=[
            pltpu.VMEM((4,) + shape[:3] + (rows, shape[4]), bf16), pltpu.SemaphoreType.DMA((len(blocks),))
        ],
        compiler_params=kernel_room,
        cost_estimate=light,
    )(grads, *blocks)


def inner_kernel(n_seq, spot, own, other, order, slope_q, slope_p, inner_q, inner_p):
    found = jnp.concatenate([own[...], other[...]], axis=1)
    hidden = jnp.zeros_like(found)
    for _ in range(3):
        piece = found.astype(bf16)
        hidden = hidden + jnp.dot(piece, order[...], preferred_element_type=f32)
        found = found - piece.astype(f32)
    first_row = 0
    for slope, inner in ((slope_q, inner_q), (slope_p, inner_p)):
        row = lax.broadcasted_iota(jnp.int32, (slope.shape[0], 1), 0) + first_row
        spread_out = jnp.zeros(slope.shape, f32)
        for k in range(n_seq):
            inside = (row >= spot[head + k]) & (row < spot[head + n_seq + k])
            spread_out = jnp.where(inside, hidden[k : k + 1, :], spread_out)
        inner[...] = (slope[...] * spread_out).astype(bf16)
        first_row += slope.shape[0]


def inner_of(spot, own, other, order, slope_q, slope_p, n_seq):
    return pl.pallas_call(
        lambda *refs: inner_kernel(n_seq, *refs),
        out_shape=(jax.ShapeDtypeStruct(slope_q.shape, bf16), jax.ShapeDtypeStruct(slope_p.shape, bf16)),
        in_specs=[in_smem] + [in_vmem] * 5,
        out_specs=(in_vmem,) * 2,
        compiler_params=kernel_room,
        cost_estimate=light,
    )(spot, own, other, order, slope_q, slope_p)


def spread(block, axes, count):
    return lax.all_to_all(jnp.broadcast_to(block[None], (count,) + block.shape), axes, 0, 0)


def per_device(sizes, query_cache, passage_cache, positive, query_tokens, passage_tokens,
               query_lengths, passage_lengths, norm_gain, adapter_down, adapter_up):
    nx, nyl, nz, nyh, nc = sizes
    n_all = nx * nyl * nz * nyh * nc
    n_pb, n_pa = nx * nyl, nz * nyh * nc
    x_i, yl_i, z_i, yh_i, c_i = (lax.axis_index(a) for a in everyone)
    first_core = c_i == 0
    own_queries, own_passages = query_cache[0], passage_cache[0]
    width = own_queries.shape[1]
    qrow, prow = own_queries.shape[0], own_passages.shape[0]
    d_own, hidden_width = adapter_down.shape
    r_own = adapter_up.shape[0]
    q_seqs, p_seqs = query_lengths.shape[-1], passage_lengths.shape[-1]

    chips = ("x", "yl", "z", "yh")
    n_chips = n_all // nc
    gain = norm_gain.astype(f32)
    gained_down = (adapter_down.astype(f32) * gain[:, None]).astype(bf16)
    (q_next, p_next, gained_down, adapter_up, query_lengths, passage_lengths, yl_i, yh_i, c_i) = barrier(
        (swap(own_queries, "yh"), swap(own_passages, "yl"), gained_down, adapter_up,
         query_lengths, passage_lengths, yl_i, yh_i, c_i)
    )

    q_pair = jnp.concatenate([own_queries, q_next], axis=0)
    p_pair = jnp.concatenate([own_passages, p_next], axis=0)
    q_before, q_after = ring_sides(q_pair, "z")
    p_before, p_after = ring_sides(p_pair, "x")
    q_blocks = [q_pair, q_before, *ring_far(q_before, q_after, "z"), q_after]
    p_blocks = [p_pair, p_before, *ring_far(p_before, p_after, "x"), p_after]
    p_other = swap(p_pair, "c")

    tok_q, tok_p = query_tokens[0, 0], passage_tokens[0, 0]
    lengths = jnp.concatenate([query_lengths[0, 0], passage_lengths[0, 0]], axis=0)
    n_seq = lengths.shape[0]
    pad = -n_seq % 8
    n_seq8 = n_seq + pad
    ends = jnp.cumsum(lengths)
    spot = jnp.concatenate([jnp.stack([yl_i, yh_i, c_i, x_i, z_i]), ends - lengths, ends]).astype(jnp.int32)

    here = jnp.arange(hidden_width, dtype=jnp.int32)
    unit, rest = here % r_own, here // r_own
    yh_s, rest = rest % nyh, rest // nyh
    z_s, rest = rest % nz, rest // nz
    yl_s, rest = rest % nyl, rest // nyl
    x_s, c_s = lax.rem(x_i - rest % nx + nx, nx), lax.rem(c_i + rest // nx, nc)
    place = ((((x_s * nyl + yl_s) * nz + z_s) * nyh + yh_s) * nc + c_s) * r_own + unit
    order = (place[:, None] == here[None, :]).astype(bf16)

    q_blocks, p_blocks, p_other, spot, order, gained_down, adapter_up = barrier(
        (q_blocks, p_blocks, p_other, spot, order, gained_down, adapter_up)
    )
    near = spread(
        jnp.concatenate([gained_down, adapter_up.reshape(-1, hidden_width)], axis=0),
        ("yl", "z", "yh"), nyl * nz * nyh,
    ).reshape(nyl, nz, nyh, -1, hidden_width)
    p_blocks = barrier(p_blocks + [p_other] + [swap(b, "c") for b in p_blocks[1:]])

    scores, local_top, local_sum = score_block(q_blocks, p_blocks)

    m_i = z_i * nyh + yh_i
    groups = nz * nyh
    step = jnp.arange(groups, dtype=jnp.int32)
    owner = lax.rem(z_i - step // nyh + nz, nz) * nyh + lax.rem(yh_i - step % nyh + nyh, nyh)
    pick = owner[:, None] == step[None, :]

    def to_owner(v):
        return jnp.sum(jnp.where(pick[:, :, None], v.reshape(groups, 1, qrow), 0), axis=0)

    def to_step(v):
        return jnp.sum(jnp.where(pick[:, :, None], v.reshape(1, groups, qrow), 0), axis=1).reshape(-1)

    packet = jnp.concatenate(
        [to_owner(local_top).reshape(-1), to_owner(local_sum).reshape(-1), positive[0].astype(f32)]
    )
    packet = jnp.pad(packet, (0, -packet.shape[0] % 128))
    packet, near = barrier((packet, near))
    near_down, near_up = near[:, :, :, :d_own], near[:, :, :, d_own:]
    down_before, down_after = ring_sides(near_down, "x")
    up_before, up_after = ring_sides(near_up, "x")
    stats = spread(packet, ("z", "yh"), groups)

    stats, down_before, down_after = barrier((stats, down_before, down_after))
    down_far = ring_far(down_before, down_after, "x")
    n_q = groups * qrow
    tops, sums = stats[:, :n_q], stats[:, n_q : 2 * n_q]
    row_top = jnp.max(tops, axis=0)
    row_sum = jnp.sum(sums * jnp.exp(tops - row_top[None, :]), axis=0)
    target = stats[:, 2 * n_q : 2 * n_q + qrow]
    stat = jnp.stack([to_step(row_top), to_step(row_sum), to_step(target)], axis=1)

    core_step = jnp.arange(nc, dtype=jnp.int32)[:, None, None, None]
    x_step = jnp.arange(nx, dtype=jnp.int32)[None, :, None, None]
    yl_step = jnp.arange(nyl, dtype=jnp.int32)[None, None, :, None]
    lane = jnp.arange(prow, dtype=jnp.int32)[None, None, None, :]
    a_of = m_i * nc + lax.rem(c_i + core_step, nc)
    b_of = lax.rem(x_i - x_step + nx, nx) * nyl + lax.rem(yl_i - yl_step + nyl, nyl)
    columns = (a_of * (n_pb * prow) + b_of * prow + lane).reshape(-1)

    coupling, q_few, p_few = couple(
        spot, scores, stat, columns[None, :], q_blocks, p_blocks, sizes, (q_seqs, qrow, p_seqs, prow)
    )
    p_few = lax.all_to_all(p_few, ("x", "yl", "c"), 0, 0)
    q_few = lax.all_to_all(q_few, ("z", "yh"), 0, 0)

    q_part = grad_parts(coupling, p_blocks, nz, False)
    coupling, q_few, q_part, up_before, up_after = barrier((coupling, q_few, q_part, up_before, up_after))
    p_part = grad_parts(coupling, q_blocks, nc * nx, True)
    p_keep, p_give = p_part[:nx], p_part[nx:]

    p_few, p_keep, p_give, down_far, up_before, up_after, q_terms = barrier(
        (p_few, p_keep, p_give, down_far, up_before, up_after, ring_sum(q_part, "z", nz))
    )
    up_far = ring_far(up_before, up_after, "x")
    down_x = [near_down, down_before, *down_far, down_after]
    up_x = [near_up, up_before, *up_far, up_after]

    p_sum = core_add(p_keep, [swap(b, "c") for b in p_give])
    down_blocks, p_sum, up_x = barrier((down_x + [swap(b, "c") for b in down_x], p_sum, up_x))
    slope_q, slope_p, active_sums = token_half(spot, down_blocks, tok_q, tok_p, n_seq, n_seq8)
    r_block, d_block = hidden_width // n_pb, width // n_pa
    sum_blocks = active_sums.astype(bf16).reshape(n_seq8, n_pb, r_block).transpose(1, 0, 2)
    sum_blocks = jnp.pad(sum_blocks, ((0, 0), (0, 0), (0, -r_block % 128)))
    q_few = jnp.sum(q_few.astype(f32), axis=0).astype(bf16)
    p_few = jnp.sum(p_few.astype(f32), axis=0).astype(bf16)

    emb_grads = jnp.concatenate([q_few, p_few], axis=0).astype(f32)
    seq_grads = (emb_grads / lengths.astype(f32)[:, None]).astype(bf16)
    seq_grads = jnp.pad(seq_grads, ((0, pad), (0, 0)))

    grad_blocks = seq_grads.reshape(n_seq8, n_pa, d_block).transpose(1, 0, 2)
    packet = jnp.concatenate(
        [
            jnp.broadcast_to(grad_blocks[None], (n_pb,) + grad_blocks.shape),
            jnp.broadcast_to(sum_blocks[:, None], (n_pb, n_pa) + sum_blocks.shape[1:]),
        ],
        axis=-1,
    ).reshape(n_all, n_seq8, -1)

    seq_both = jnp.concatenate([seq_grads, swap(seq_grads, "c")], axis=0)
    p_terms = ring_sum(p_sum, "x", nx)

    hidden = hidden_of(seq_both, up_x, r_own * width // hidden_width, hidden_width // nc)
    inner_q, inner_p = inner_of(
        spot, hidden[:n_seq8], swap(hidden[n_seq8:], "c"), order, slope_q, slope_p, n_seq
    )
    inner_q, inner_p, p_terms, packet = barrier((inner_q, inner_p, p_terms, packet))
    everything = lax.all_to_all(packet, everyone, 0, 0).reshape(n_all * n_seq8, -1)
    q_own, q_away = ring_add(q_terms)
    p_own, p_away = ring_add(p_terms)
    keep, give = down_parts(spot, tok_q, tok_p, inner_q, inner_p, d_own)
    keep, give, q_own, q_away, p_own, p_away, everything = barrier(
        (keep, give, q_own, q_away, p_own, p_away, everything)
    )
    chip_sum = chip_add(keep, [swap(b, "c") for b in give])
    up_block = lax.dot_general(
        everything[:, d_block : d_block + r_block], everything[:, :d_block], turned, preferred_element_type=f32
    ).reshape(nz, nyh, nc, r_own, 1, d_block)

    def trade(block, axis, index):
        first = index == 0
        mine = jnp.where(first, block[..., 0, :, :, :], block[..., 1, :, :, :])
        theirs = swap(jnp.where(first, block[..., 1, :, :, :], block[..., 0, :, :, :]), axis)
        return jnp.concatenate(
            [jnp.where(first, mine, theirs), jnp.where(first, theirs, mine)], axis=-2
        )

    up_block = trade(trade(up_block, "c", c_i), "yh", yh_i)
    z_blocks = [lax.dynamic_index_in_dim(up_block, lax.rem(z_i + k, nz), 0, keepdims=False) for k in range(nz)]
    z_blocks = [z_blocks[0]] + [shift(z_blocks[k], "z", k, nz) for k in range(1, nz)]
    chip_sum, z_blocks = barrier((chip_sum, z_blocks))
    query_grad = (q_own + swap(q_away, "yh").astype(f32)).astype(bf16)
    passage_grad = (p_own + swap(p_away, "yl").astype(f32)).astype(bf16)
    arrived = lax.all_to_all(chip_sum, chips, 0, 0)

    up_grad = jnp.zeros((r_own, nz) + up_block.shape[2:], f32)
    for k in range(nz):
        up_grad = lax.dynamic_update_slice_in_dim(
            up_grad, z_blocks[k][:, None], lax.rem(z_i - k + nz, nz), axis=1
        )
    up_grad = up_grad.reshape(r_own, width)

    ungained = jnp.sum(arrived.astype(f32), axis=0)
    down_grad = ungained * gain[:, None]
    gain_grad = jnp.sum(ungained * adapter_down.astype(f32), axis=1)
    return (query_grad[None], passage_grad[None], down_grad, up_grad, gain_grad)


def solution(mesh):
    nyl, nyh, nc = 2, 2, 2
    nx, nz = mesh.shape["pb"] // nyl, mesh.shape["pa"] // (nyh * nc)
    sizes = (nx, nyl, nz, nyh, nc)
    fine = Mesh(mesh.devices.reshape(sizes), everyone)
    pb, pa = ("x", "yl"), ("z", "yh", "c")
    in_specs = (
        P(pb, pa, None),
        P(pa, pb, None),
        P(pb, pa),
        P(pb, pa, None, None),
        P(pa, pb, None, None),
        P(pb, pa, None),
        P(pa, pb, None),
        P(everyone),
        P(everyone, None),
        P(everyone, None),
    )
    out_specs = (P(pb, pa, None), P(pa, pb, None), P(everyone, None), P(everyone, None), P(everyone))

    def body(*args):
        return per_device(sizes, *args)

    return jax.shard_map(body, mesh=fine, in_specs=in_specs, out_specs=out_specs, check_vma=False)
```

profile of v0, /device:TPU:0, one launch (start us, length us, event | category | flops | bytes accessed | tf_op | source)
XLA Modules:
  0.0 252.4 jit_solution(509441508175215985)
XLA Ops:
  0.7 3.4 %collective-permute-start = (bf16[32,4096]{1,0:T(8,128)(2,1)}, bf16[32,4096]{1,0:T(8,128)(2,1)S(1)}, u32[]{:S(2)}, u32[]{:S(2)}) collective-permute-start(bf16[32,4096]{1,0:T(8,128)(2,1)} %bitcast.70), channel_id=1, source_target_pairs={{0,2},{2,0},{1,3},{3,1},{4,6},{6,4},{5,7},{7,5},{8,10},{10,8},{9,1... | collective-permute-start | bytes 786440 | tf_op jit(solution)/shard_map/ppermute | solution.py:22
  6.2 5.5 %collective-permute-done = bf16[32,4096]{1,0:T(8,128)(2,1)S(1)} collective-permute-done((bf16[32,4096]{1,0:T(8,128)(2,1)}, bf16[32,4096]{1,0:T(8,128)(2,1)S(1)}, u32[]{:S(2)}, u32[]{:S(2)}) %collective-permute-start) | collective-permute-done | bytes 262176 | tf_op jit(solution)/shard_map/ppermute | solution.py:22
  11.6 4.9 %collective-permute-done.1 = bf16[32,4096]{1,0:T(8,128)(2,1)S(1)} collective-permute-done((bf16[32,4096]{1,0:T(8,128)(2,1)}, bf16[32,4096]{1,0:T(8,128)(2,1)S(1)}, u32[]{:S(2)}, u32[]{:S(2)}) %collective-permute-start.1) | collective-permute-done | bytes 262176 | tf_op jit(solution)/shard_map/ppermute | solution.py:22
  26.3 5.3 %collective-permute-done.6.refs_6_.refs_10_.refs_2_ = bf16[64,4096]{1,0:T(8,128)(2,1)S(1)} collective-permute-done((bf16[64,4096]{1,0:T(8,128)(2,1)S(1)}, bf16[64,4096]{1,0:T(8,128)(2,1)S(1)}, u32[]{:S(2)}, u32[]{:S(2)}) %collective-permute-start.6) | collective-permute-done | bytes 524320 | tf_op jit(solution)/shard_map/ppermute | solution.py:18
  33.5 3.0 %collective-permute-start.9 = (bf16[32,4096]{1,0:T(8,128)(2,1)}, bf16[32,4096]{1,0:T(8,128)(2,1)}, u32[]{:S(2)}, u32[]{:S(2)}) collective-permute-start(bf16[32,4096]{1,0:T(8,128)(2,1)} %slice.91), channel_id=1, source_target_pairs={{0,96},{32,0},{64,32},{96,64},{1,97},{33,1},{65,33},{97,65},{2,98}... | collective-permute-start | bytes 786440 | tf_op jit(solution)/shard_map/ppermute | solution.py:18
  48.6 6.3 %all-to-all-start = ((bf16[16,64,512]{2,1,0:T(8,128)(2,1)}), bf16[16,64,512]{2,1,0:T(8,128)(2,1)}, u32[]{:S(2)}, u32[]{:S(2)}) async-start(bf16[16,64,512]{2,1,0:T(8,128)(2,1)} %broadcast_in_dim.139), calls=%async_computation | async-start | bytes 2097152 | tf_op jit(solution)/shard_map/all_to_all | solution.py:529
  60.2 5.1 %shard_map.137 = (f32[256,512]{1,0:T(8,128)}, f32[256,1]{1,0:T(8,128)}, f32[256,1]{1,0:T(8,128)}) custom-call(bf16[64,4096]{1,0:T(8,128)(2,1)} %copy-done.6, bf16[64,4096]{1,0:T(8,128)(2,1)} %copy-done.7, bf16[32,4096]{1,0:T(8,128)(2,1)} %collective-permute-done.3.refs_2_.refs_6_.refs_3_, bf16[32,4096]{1,0:T(8,128)(2,1)} %collective-permute-done.5.refs_3_.refs_7_.refs_4_, ...), custom_call_target="tpu_custom_call" | custom-call | tf_op jit(solution)/shard_map/pallas_call | solution.py:112
  69.5 3.2 %collective-permute-start.16 = (bf16[2,4,2,32,512]{4,3,2,1,0:T(8,128)(2,1)S(1)}, bf16[2,4,2,32,512]{4,3,2,1,0:T(8,128)(2,1)S(1)}, u32[]{:S(2)}, u32[]{:S(2)}) collective-permute-start(bf16[2,4,2,32,512]{4,3,2,1,0:T(8,128)(2,1)S(1)} %get-tuple-element.233.refs_1_), channel_id=1, source_target_pairs={{0,96},{32,0},{64,32},{96,64},{1,97},{33,1},{65,33},{97,65},{2,98}... | collective-permute-start | bytes 1572872 | tf_op jit(solution)/shard_map/ppermute | solution.py:18
  73.5 6.7 %all-to-all-start.1 = ((f32[8,1,640]{2,1,0:T(1,128)}), f32[8,1,640]{2,1,0:T(1,128)S(1)}, u32[]{:S(2)}, u32[]{:S(2)}) async-start(f32[8,1,640]{2,1,0:T(1,128)} %broadcast_in_dim.140), calls=%async_computation.1 | async-start | bytes 40960 | tf_op jit(solution)/shard_map/all_to_all | solution.py:529
  80.9 3.2 %collective-permute-start.18 = (bf16[2,4,2,32,512]{4,3,2,1,0:T(8,128)(2,1)S(1)}, bf16[2,4,2,32,512]{4,3,2,1,0:T(8,128)(2,1)S(1)}, u32[]{:S(2)}, u32[]{:S(2)}) collective-permute-start(bf16[2,4,2,32,512]{4,3,2,1,0:T(8,128)(2,1)S(1)} %get-tuple-element.227.refs_1_), channel_id=1, source_target_pairs={{0,96},{32,0},{64,32},{96,64},{1,97},{33,1},{65,33},{97,65},{2,98}... | collective-permute-start | bytes 1572872 | tf_op jit(solution)/shard_map/ppermute | solution.py:18
  84.1 3.7 %all-to-all-done.1 = f32[8,1,640]{2,1,0:T(1,128)S(1)} async-done(((f32[8,1,640]{2,1,0:T(1,128)}), f32[8,1,640]{2,1,0:T(1,128)S(1)}, u32[]{:S(2)}, u32[]{:S(2)}) %all-to-all-start.1) | async-done | bytes 20512 | tf_op jit(solution)/shard_map/all_to_all | solution.py:529
  89.3 6.3 %shard_map.138 = (bf16[256,512]{1,0:T(8,128)(2,1)}, bf16[8,4,4096]{2,1,0:T(4,128)(2,1)}, bf16[16,2,4096]{2,1,0:T(2,128)(2,1)}) custom-call(s32[17]{0:T(128)} %concatenate.40.refs_0_.core, f32[256,512]{1,0:T(8,128)} %get-tuple-element.177.refs_1_, f32[256,3]{1,0:T(8,128)} %copy.42.refs_2_, s32[1,512]{1,0:T(1,128)} %add.343.refs_3_, ...), custom_call_target="tpu_custom_call" | custom-call | tf_op jit(solution)/shard_map/pallas_call | solution.py:167
  95.7 3.8 %all-to-all-start.2 = ((bf16[8,4,4096]{2,1,0:T(4,128)(2,1)}), bf16[8,4,4096]{2,1,0:T(4,128)(2,1)S(1)}, u32[]{:S(2)}, u32[]{:S(2)}) async-start(bf16[8,4,4096]{2,1,0:T(4,128)(2,1)} %get-tuple-element.186), calls=%async_computation.2 | async-start | bytes 524288 | tf_op jit(solution)/shard_map/all_to_all | solution.py:634
  100.2 4.4 %shard_map.139 = (bf16[64,4096]{1,0:T(8,128)(2,1)}, bf16[64,4096]{1,0:T(8,128)(2,1)}, bf16[64,4096]{1,0:T(8,128)(2,1)}, bf16[64,4096]{1,0:T(8,128)(2,1)}) custom-call(bf16[256,512]{1,0:T(8,128)(2,1)} %get-tuple-element.193.refs_0_, bf16[64,4096]{1,0:T(8,128)(2,1)} %copy-done, bf16[64,4096]{1,0:T(8,128)(2,1)} %copy-done.1, bf16[32,4096]{1,0:T(8,128)(2,1)} %copy-done.8, ...), custom_call_target="tpu_custom_call" | custom-call | flops 1073741824 | bytes 6291456 | tf_op jit(solution)/shard_map/pallas_call | solution.py:283
  104.6 3.6 %all-to-all-done.2 = bf16[8,4,4096]{2,1,0:T(4,128)(2,1)S(1)} async-done(((bf16[8,4,4096]{2,1,0:T(4,128)(2,1)}), bf16[8,4,4096]{2,1,0:T(4,128)(2,1)S(1)}, u32[]{:S(2)}, u32[]{:S(2)}) %all-to-all-start.2) | async-done | bytes 262176 | tf_op jit(solution)/shard_map/all_to_all | solution.py:634
  111.5 3.0 %collective-permute-start.20 = (bf16[1,4,2,32,512]{4,3,2,1,0:T(8,128)(2,1)}, bf16[1,4,2,32,512]{4,3,2,1,0:T(8,128)(2,1)S(1)}, u32[]{:S(2)}, u32[]{:S(2)}) collective-permute-start(bf16[1,4,2,32,512]{4,3,2,1,0:T(8,128)(2,1)} %slice.77), channel_id=1, source_target_pairs={{0,96},{32,0},{64,32},{96,64},{1,97},{33,1},{65,33},{97,65},{2,98}... | collective-permute-start | bytes 786440 | tf_op jit(solution)/shard_map/ppermute | solution.py:18
  114.4 3.5 %all-to-all-start.3 = ((bf16[16,2,4096]{2,1,0:T(2,128)(2,1)}), bf16[16,2,4096]{2,1,0:T(2,128)(2,1)S(1)}, u32[]{:S(2)}, u32[]{:S(2)}) async-start(bf16[16,2,4096]{2,1,0:T(2,128)(2,1)} %get-tuple-element.192), calls=%async_computation.3 | async-start | bytes 524288 | tf_op jit(solution)/shard_map/all_to_all | solution.py:633
  118.0 4.2 %shard_map.140 = (bf16[64,4096]{1,0:T(8,128)(2,1)}, bf16[64,4096]{1,0:T(8,128)(2,1)}, bf16[64,4096]{1,0:T(8,128)(2,1)}, bf16[64,4096]{1,0:T(8,128)(2,1)}, bf16[6...) custom-call(bf16[256,512]{1,0:T(8,128)(2,1)} %get-tuple-element.193.refs_0_,, ...), custom_call_target="tpu_custom_call" | custom-call | flops 1073741824 | bytes 6291456 | tf_op jit(solution)/shard_map/pallas_call | solution.py:283
  125.8 7.5 %collective-permute-done.23.refs_3_ = bf16[64,4096]{1,0:T(8,128)(2,1)} collective-permute-done((bf16[64,4096]{1,0:T(8,128)(2,1)}, bf16[64,4096]{1,0:T(8,128)(2,1)}, u32[]{:S(2)}, u32[]{:S(2)}) %collective-permute-start.23) | collective-permute-done | bytes 524320 | tf_op jit(solution)/shard_map/ppermute | solution.py:18
  136.3 2.4 collective-permute-start.35
  140.1 3.3 %shard_map.141 = (bf16[64,4096]{1,0:T(8,128)(2,1)}, bf16[64,4096]{1,0:T(8,128)(2,1)}, bf16[64,4096]{1,0:T(8,128)(2,1)}, bf16[64,4096]{1,0:T(8,128)(2,1)}) custom-call(bf16[64,4096]{1,0:T(8,128)(2,1)} %get-tuple-element.213.refs_0_, bf16[64,4096]{1,0:T(8,128)(2,1)} %get-tuple-element.214.refs_1_, bf16[64,4096]{1,0:T(8,128)(2,1)} %get-tuple-element.215.refs_2_, ...), custom_call_target="tpu_custom_call" | custom-call | tf_op jit(solution)/shard_map/pallas_call | solution.py:223
  145.2 2.8 %collective-permute-start.37 = (bf16[64,4096]{1,0:T(8,128)(2,1)}, bf16[64,4096]{1,0:T(8,128)(2,1)S(1)}, u32[]{:S(2)}, u32[]{:S(2)}) collective-permute-start(bf16[64,4096]{1,0:T(8,128)(2,1)} %get-tuple-element.248), channel_id=1, source_target_pairs={{0,96},{32,0},{64,32},{96,64},{1,97},{33,1},{65,33},{97,65},{2,98}... | collective-permute-start | bytes 1572872 | tf_op jit(solution)/shard_map/ppermute | solution.py:18
  149.8 11.3 %shard_map.143 = (f32[128,512]{1,0:T(8,128)}, f32[768,512]{1,0:T(8,128)}, f32[8,512]{1,0:T(8,128)}) custom-call(s32[17]{0:T(128)} %concatenate.40.refs_0_.core, bf16[2,4,2,32,512]{4,3,2,1,0:T(8,128)(2,1)} %copy-done.12, bf16[2,4,2,32,512]{4,3,2,1,0:T(8,128)(2,1)} %copy-done.13, bf16[1,4,2,32,512]{4,3,2,1,0:T(8,128)(2,1)} %collective-permute-done.19.refs_3_, ...), custom_call_target="tpu_custom_call" | custom-call | tf_op jit(solution)/shard_map/pallas_call | solution.py:425
  161.9 4.5 %shard_map.142 = f32[16,256]{1,0:T(8,128)} custom-call(bf16[16,4096]{1,0:T(8,128)(2,1)} %pad_maximum_fusion.3.refs_0_, bf16[2,4,2,32,512]{4,3,2,1,0:T(8,128)(2,1)} %copy-done.11, bf16[2,4,2,32,512]{4,3,2,1,0:T(8,128)(2,1)} %copy-done.15, bf16[1,4,2,32,512]{4,3,2,1,0:T(8,128)(2,1)} %copy-done.29, bf16[1,4,2,32,512]{4,3,2,1,0:T(8,128)(2,1)} %copy-done.30, ...), custom_call_target="tpu_custom_call" | custom-call | tf_op jit(solution)/shard_map/pallas_call | solution.py:486
  169.5 4.2 %shard_map.144 = (bf16[128,512]{1,0:T(8,128)(2,1)}, bf16[768,512]{1,0:T(8,128)(2,1)}) custom-call(s32[17]{0:T(128)} %concatenate.40.refs_0_.core, f32[8,256]{1,0:T(8,128)} %get-tuple-element.311.refs_1_, f32[8,256]{1,0:T(8,128)} %copy-done.35, bf16[512,512]{1,0:T(8,128)(2,1)} %fusion.refs_3_, f32[128,512]{1,0:T(8,128)} %get-tuple-element.243.refs_4_, ...), custom_call_target="tpu_custom_call" | custom-call | tf_op jit(solution)/shard_map/pallas_call | solution.py:518
  173.8 7.9 %all-to-all-start.4 = ((bf16[128,8,384]{2,1,0:T(8,128)(2,1)}), bf16[128,8,384]{2,1,0:T(8,128)(2,1)S(1)}, u32[]{:S(2)}, u32[]{:S(2)}) async-start(bf16[128,8,384]{2,1,0:T(8,128)(2,1)} %bitcast.18), calls=%async_computation.4 | async-start | bytes 1572864 | tf_op jit(solution)/shard_map/all_to_all | solution.py:678
  186.4 9.3 %shard_map.145 = (bf16[64,32,512]{2,1,0:T(8,128)(2,1)}, bf16[16,32,512]{2,1,0:T(8,128)(2,1)}, bf16[16,32,512]{2,1,0:T(8,128)(2,1)}, bf16[16,32,512]{2,1,0:T(8,128)(2,1)}, bf16[16,32,512]{2,1,0:T(8,128)(2,1)}) custom-call(s32[17]{0:T(128)} %concatenate.40.refs_0_.core, bf16[128,4096]{1,0:T(8,128)(2,1)} %bitcast.66, bf16[768,4096]{1,0:T(8,128)(2,1)} %bitcast.63, ...), custom_call_target="tpu_custom_call" | custom-call | flops 3758096384 | bytes 8388608 | tf_op jit(solution)/shard_map/pallas_call | solution.py:337
  200.9 4.4 %collective-permute-done.47 = f32[4,4,2,256]{3,2,1,0:T(2,128)S(1)} collective-permute-done((f32[4,4,2,256]{3,2,1,0:T(2,128)S(1)}, f32[4,4,2,256]{3,2,1,0:T(2,128)S(1)}, u32[]{:S(2)}, u32[]{:S(2)}) %collective-permute-start.47) | collective-permute-done | bytes 32800 | tf_op jit(solution)/shard_map/ppermute | solution.py:22
  210.2 2.8 %collective-permute-start.40 = (bf16[32,4096]{1,0:T(8,128)(2,1)}, bf16[32,4096]{1,0:T(8,128)(2,1)}, u32[]{:S(2)}, u32[]{:S(2)}) collective-permute-start(bf16[32,4096]{1,0:T(8,128)(2,1)} %get-tuple-element.273), channel_id=1, source_target_pairs={{0,2},{2,0},{1,3},{3,1},{4,6},{6,4},{5,7},{7,5},{8,10},{10,8},{9,1... | collective-permute-start | bytes 786440 | tf_op jit(solution)/shard_map/ppermute | solution.py:22
  213.0 3.4 %shard_map.148 = bf16[64,32,512]{2,1,0:T(8,128)(2,1)} custom-call(bf16[64,32,512]{2,1,0:T(8,128)(2,1)} %get-tuple-element.276.refs_0_, bf16[16,32,512]{2,1,0:T(8,128)(2,1)} %copy-done.17, bf16[16,32,512]{2,1,0:T(8,128)(2,1)} %copy-done.18, bf16[16,32,512]{2,1,0:T(8,128)(2,1)} %copy-done.19, bf16[16,32,512]{2,1,0:T(8,128)(2,1)} %copy-done.20), custom_call_target="tpu_custom_call" | custom-call | tf_op jit(solution)/shard_map/pallas_call | solution.py:249
  216.5 5.9 %all-to-all-start.5 = ((bf16[64,32,512]{2,1,0:T(8,128)(2,1)}), bf16[64,32,512]{2,1,0:T(8,128)(2,1)S(1)}, u32[]{:S(2)}, u32[]{:S(2)}) async-start(bf16[64,32,512]{2,1,0:T(8,128)(2,1)} %shard_map.148), calls=%async_computation.5 | async-start | bytes 4194304 | tf_op jit(solution)/shard_map/all_to_all | solution.py:704
  225.7 25.1 %all-to-all-done.5 = bf16[64,32,512]{2,1,0:T(8,128)(2,1)S(1)} async-done(((bf16[64,32,512]{2,1,0:T(8,128)(2,1)}), bf16[64,32,512]{2,1,0:T(8,128)(2,1)S(1)}, u32[]{:S(2)}, u32[]{:S(2)}) %all-to-all-start.5) | async-done | bytes 2097184 | tf_op jit(solution)/shard_map/all_to_all | solution.py:704
  (256 shorter events, 77.2 us)
Async XLA Ops:
  0.7 11.0 %collective-permute-start = (bf16[32,4096]{1,0:T(8,128)(2,1)}, bf16[32,4096]{1,0:T(8,128)(2,1)S(1)}, u32[]{:S(2)}, u32[]{:S(2)}) collective-permute-start(bf16[32,4096]{1,0:T(8,128)(2,1)} %bitcast.70), channel_id=1, source_target_pairs={{0,2},{2,0},{1,3},{3,1},{4,6},{6,4},{5,7},{7,5},{8,10},{10,8},{9,1... | collective-permute-start | bytes 786440 | tf_op jit(solution)/shard_map/ppermute | solution.py:22
  4.0 12.5 %collective-permute-start.1 = (bf16[32,4096]{1,0:T(8,128)(2,1)}, bf16[32,4096]{1,0:T(8,128)(2,1)S(1)}, u32[]{:S(2)}, u32[]{:S(2)}) collective-permute-start(bf16[32,4096]{1,0:T(8,128)(2,1)} %bitcast.68), channel_id=1, source_target_pairs={{0,16},{16,0},{1,17},{17,1},{2,18},{18,2},{3,19},{19,3},{4,20},{20... | collective-permute-start | bytes 786440 | tf_op jit(solution)/shard_map/ppermute | solution.py:22
  17.5 14.1 %collective-permute-start.6 = (bf16[64,4096]{1,0:T(8,128)(2,1)S(1)}, bf16[64,4096]{1,0:T(8,128)(2,1)S(1)}, u32[]{:S(2)}, u32[]{:S(2)}) collective-permute-start(bf16[64,4096]{1,0:T(8,128)(2,1)S(1)} %pad_maximum_fusion.2.refs_5_.refs_9_.refs_1_), channel_id=1, source_target_pairs={{0,32},{32,64},{64,96},{96,0},{1,33},{33,65},{65,97},{97,1},{2,34}... | collective-permute-start | bytes 1572872 | tf_op jit(solution)/shard_map/ppermute | solution.py:18
  19.1 13.6 %collective-permute-start.8 = (bf16[64,4096]{1,0:T(8,128)(2,1)S(1)}, bf16[64,4096]{1,0:T(8,128)(2,1)S(1)}, u32[]{:S(2)}, u32[]{:S(2)}) collective-permute-start(bf16[64,4096]{1,0:T(8,128)(2,1)S(1)} %pad_maximum_fusion.2.refs_5_.refs_9_.refs_1_), channel_id=1, source_target_pairs={{0,96},{32,0},{64,32},{96,64},{1,97},{33,1},{65,33},{97,65},{2,98}... | collective-permute-start | bytes 1572872 | tf_op jit(solution)/shard_map/ppermute | solution.py:18
  21.8 14.6 %collective-permute-start.2 = (bf16[64,4096]{1,0:T(8,128)(2,1)S(1)}, bf16[64,4096]{1,0:T(8,128)(2,1)S(1)}, u32[]{:S(2)}, u32[]{:S(2)}) collective-permute-start(bf16[64,4096]{1,0:T(8,128)(2,1)S(1)} %pad_maximum_fusion.1.refs_0_.refs_4_.refs_1_), channel_id=1, source_target_pairs={{0,4},{4,8},{8,12},{12,0},{1,5},{5,9},{9,13},{13,1},{2,6},{6,10},{... | collective-permute-start | bytes 1572872 | tf_op jit(solution)/shard_map/ppermute | solution.py:18
  23.8 15.3 %collective-permute-start.4 = (bf16[64,4096]{1,0:T(8,128)(2,1)S(1)}, bf16[64,4096]{1,0:T(8,128)(2,1)}, u32[]{:S(2)}, u32[]{:S(2)}) collective-permute-start(bf16[64,4096]{1,0:T(8,128)(2,1)S(1)} %pad_maximum_fusion.1.refs_0_.refs_4_.refs_1_), channel_id=1, source_target_pairs={{0,12},{4,0},{8,4},{12,8},{1,13},{5,1},{9,5},{13,9},{2,14},{6,2},{... | collective-permute-start | bytes 1572872 | tf_op jit(solution)/shard_map/ppermute | solution.py:18
  26.0 18.5 %collective-permute-start.10 = (bf16[64,4096]{1,0:T(8,128)(2,1)S(1)}, bf16[64,4096]{1,0:T(8,128)(2,1)S(1)}, u32[]{:S(2)}, u32[]{:S(2)}) collective-permute-start(bf16[64,4096]{1,0:T(8,128)(2,1)S(1)} %pad_maximum_fusion.2.refs_5_.refs_9_.refs_1_), channel_id=1, source_target_pairs={{0,1},{1,0},{2,3},{3,2},{4,5},{5,4},{6,7},{7,6},{8,9},{9,8},{10,11... | collective-permute-start | bytes 1572872 | tf_op jit(solution)/shard_map/ppermute | solution.py:22
  32.4 12.1 %collective-permute-start.7 = (bf16[32,4096]{1,0:T(8,128)(2,1)}, bf16[32,4096]{1,0:T(8,128)(2,1)S(1)}, u32[]{:S(2)}, u32[]{:S(2)}) collective-permute-start(bf16[32,4096]{1,0:T(8,128)(2,1)} %slice.90), channel_id=1, source_target_pairs={{0,32},{32,64},{64,96},{96,0},{1,33},{33,65},{65,97},{97,1},{2,34}... | collective-permute-start | bytes 786440 | tf_op jit(solution)/shard_map/ppermute | solution.py:18
  33.5 11.1 %collective-permute-start.9 = (bf16[32,4096]{1,0:T(8,128)(2,1)}, bf16[32,4096]{1,0:T(8,128)(2,1)}, u32[]{:S(2)}, u32[]{:S(2)}) collective-permute-start(bf16[32,4096]{1,0:T(8,128)(2,1)} %slice.91), channel_id=1, source_target_pairs={{0,96},{32,0},{64,32},{96,64},{1,97},{33,1},{65,33},{97,65},{2,98}... | collective-permute-start | bytes 786440 | tf_op jit(solution)/shard_map/ppermute | solution.py:18
  48.6 19.5 %all-to-all-start = ((bf16[16,64,512]{2,1,0:T(8,128)(2,1)}), bf16[16,64,512]{2,1,0:T(8,128)(2,1)}, u32[]{:S(2)}, u32[]{:S(2)}) async-start(bf16[16,64,512]{2,1,0:T(8,128)(2,1)} %broadcast_in_dim.139), calls=%async_computation | async-start | bytes 2097152 | tf_op jit(solution)/shard_map/all_to_all | solution.py:529
  69.4 18.5 %collective-permute-start.15 = (bf16[2,4,2,32,512]{4,3,2,1,0:T(8,128)(2,1)S(1)}, bf16[2,4,2,32,512]{4,3,2,1,0:T(8,128)(2,1)S(1)}, u32[]{:S(2)}, u32[]{:S(2)}) collective-permute-start(bf16[2,4,2,32,512]{4,3,2,1,0:T(8,128)(2,1)S(1)} %get-tuple-element.233.refs_1_), channel_id=1, source_target_pairs={{0,32},{32,64},{64,96},{96,0},{1,33},{33,65},{65,97},{97,1},{2,34}... | collective-permute-start | bytes 1572872 | tf_op jit(solution)/shard_map/ppermute | solution.py:18
  69.5 18.4 %collective-permute-start.16 = (bf16[2,4,2,32,512]{4,3,2,1,0:T(8,128)(2,1)S(1)}, bf16[2,4,2,32,512]{4,3,2,1,0:T(8,128)(2,1)S(1)}, u32[]{:S(2)}, u32[]{:S(2)}) collective-permute-start(bf16[2,4,2,32,512]{4,3,2,1,0:T(8,128)(2,1)S(1)} %get-tuple-element.233.refs_1_), channel_id=1, source_target_pairs={{0,96},{32,0},{64,32},{96,64},{1,97},{33,1},{65,33},{97,65},{2,98}... | collective-permute-start | bytes 1572872 | tf_op jit(solution)/shard_map/ppermute | solution.py:18
  73.5 14.4 %all-to-all-start.1 = ((f32[8,1,640]{2,1,0:T(1,128)}), f32[8,1,640]{2,1,0:T(1,128)S(1)}, u32[]{:S(2)}, u32[]{:S(2)}) async-start(f32[8,1,640]{2,1,0:T(1,128)} %broadcast_in_dim.140), calls=%async_computation.1 | async-start | bytes 40960 | tf_op jit(solution)/shard_map/all_to_all | solution.py:529
  80.9 23.7 %collective-permute-start.17 = (bf16[2,4,2,32,512]{4,3,2,1,0:T(8,128)(2,1)S(1)}, bf16[2,4,2,32,512]{4,3,2,1,0:T(8,128)(2,1)S(1)}, u32[]{:S(2)}, u32[]{:S(2)}) collective-permute-start(bf16[2,4,2,32,512]{4,3,2,1,0:T(8,128)(2,1)S(1)} %get-tuple-element.227.refs_1_), channel_id=1, source_target_pairs={{0,32},{32,64},{64,96},{96,0},{1,33},{33,65},{65,97},{97,1},{2,34}... | collective-permute-start | bytes 1572872 | tf_op jit(solution)/shard_map/ppermute | solution.py:18
  80.9 23.7 %collective-permute-start.18 = (bf16[2,4,2,32,512]{4,3,2,1,0:T(8,128)(2,1)S(1)}, bf16[2,4,2,32,512]{4,3,2,1,0:T(8,128)(2,1)S(1)}, u32[]{:S(2)}, u32[]{:S(2)}) collective-permute-start(bf16[2,4,2,32,512]{4,3,2,1,0:T(8,128)(2,1)S(1)} %get-tuple-element.227.refs_1_), channel_id=1, source_target_pairs={{0,96},{32,0},{64,32},{96,64},{1,97},{33,1},{65,33},{97,65},{2,98}... | collective-permute-start | bytes 1572872 | tf_op jit(solution)/shard_map/ppermute | solution.py:18
  95.7 12.5 %all-to-all-start.2 = ((bf16[8,4,4096]{2,1,0:T(4,128)(2,1)}), bf16[8,4,4096]{2,1,0:T(4,128)(2,1)S(1)}, u32[]{:S(2)}, u32[]{:S(2)}) async-start(bf16[8,4,4096]{2,1,0:T(4,128)(2,1)} %get-tuple-element.186), calls=%async_computation.2 | async-start | bytes 524288 | tf_op jit(solution)/shard_map/all_to_all | solution.py:634
  100.2 11.3 %collective-permute-start.19 = (bf16[1,4,2,32,512]{4,3,2,1,0:T(8,128)(2,1)}, bf16[1,4,2,32,512]{4,3,2,1,0:T(8,128)(2,1)}, u32[]{:S(2)}, u32[]{:S(2)}) collective-permute-start(bf16[1,4,2,32,512]{4,3,2,1,0:T(8,128)(2,1)} %slice.76), channel_id=1, source_target_pairs={{0,32},{32,64},{64,96},{96,0},{1,33},{33,65},{65,97},{97,1},{2,34}... | collective-permute-start | bytes 786440 | tf_op jit(solution)/shard_map/ppermute | solution.py:18
  108.2 15.2 %collective-permute-start.21 = (bf16[64,4096]{1,0:T(8,128)(2,1)}, bf16[64,4096]{1,0:T(8,128)(2,1)}, u32[]{:S(2)}, u32[]{:S(2)}) collective-permute-start(bf16[64,4096]{1,0:T(8,128)(2,1)} %get-tuple-element.207), channel_id=1, source_target_pairs={{0,12},{4,0},{8,4},{12,8},{1,13},{5,1},{9,5},{13,9},{2,14},{6,2},{... | collective-permute-start | bytes 1572872 | tf_op jit(solution)/shard_map/ppermute | solution.py:18
  109.1 16.7 %collective-permute-start.22 = (bf16[64,4096]{1,0:T(8,128)(2,1)}, bf16[64,4096]{1,0:T(8,128)(2,1)}, u32[]{:S(2)}, u32[]{:S(2)}) collective-permute-start(bf16[64,4096]{1,0:T(8,128)(2,1)} %get-tuple-element.208), channel_id=1, source_target_pairs={{0,8},{4,12},{8,0},{12,4},{1,9},{5,13},{9,1},{13,5},{2,10},{6,14},... | collective-permute-start | bytes 1572872 | tf_op jit(solution)/shard_map/ppermute | solution.py:18
  110.5 22.7 %collective-permute-start.23 = (bf16[64,4096]{1,0:T(8,128)(2,1)}, bf16[64,4096]{1,0:T(8,128)(2,1)}, u32[]{:S(2)}, u32[]{:S(2)}) collective-permute-start(bf16[64,4096]{1,0:T(8,128)(2,1)} %get-tuple-element.209), channel_id=1, source_target_pairs={{0,4},{4,8},{8,12},{12,0},{1,5},{5,9},{9,13},{13,1},{2,6},{6,10},{... | collective-permute-start | bytes 1572872 | tf_op jit(solution)/shard_map/ppermute | solution.py:18
  110.8 23.0 %collective-permute-start.25 = (bf16[2,4,2,32,512]{4,3,2,1,0:T(8,128)(2,1)S(1)}, bf16[2,4,2,32,512]{4,3,2,1,0:T(8,128)(2,1)}, u32[]{:S(2)}, u32[]{:S(2)}) collective-permute-start(bf16[2,4,2,32,512]{4,3,2,1,0:T(8,128)(2,1)S(1)} %get-tuple-element.233.refs_1_), channel_id=1, source_target_pairs={{0,1},{1,0},{2,3},{3,2},{4,5},{5,4},{6,7},{7,6},{8,9},{9,8},{10,11... | collective-permute-start | bytes 1572872 | tf_op jit(solution)/shard_map/ppermute | solution.py:22
  111.5 10.9 %collective-permute-start.20 = (bf16[1,4,2,32,512]{4,3,2,1,0:T(8,128)(2,1)}, bf16[1,4,2,32,512]{4,3,2,1,0:T(8,128)(2,1)S(1)}, u32[]{:S(2)}, u32[]{:S(2)}) collective-permute-start(bf16[1,4,2,32,512]{4,3,2,1,0:T(8,128)(2,1)} %slice.77), channel_id=1, source_target_pairs={{0,96},{32,0},{64,32},{96,64},{1,97},{33,1},{65,33},{97,65},{2,98}... | collective-permute-start | bytes 786440 | tf_op jit(solution)/shard_map/ppermute | solution.py:18
  114.4 11.2 %all-to-all-start.3 = ((bf16[16,2,4096]{2,1,0:T(2,128)(2,1)}), bf16[16,2,4096]{2,1,0:T(2,128)(2,1)S(1)}, u32[]{:S(2)}, u32[]{:S(2)}) async-start(bf16[16,2,4096]{2,1,0:T(2,128)(2,1)} %get-tuple-element.192), calls=%async_computation.3 | async-start | bytes 524288 | tf_op jit(solution)/shard_map/all_to_all | solution.py:633
  122.4 12.5 %collective-permute-start.26 = (bf16[2,4,2,32,512]{4,3,2,1,0:T(8,128)(2,1)S(1)}, bf16[2,4,2,32,512]{4,3,2,1,0:T(8,128)(2,1)}, u32[]{:S(2)}, u32[]{:S(2)}) collective-permute-start(bf16[2,4,2,32,512]{4,3,2,1,0:T(8,128)(2,1)S(1)} %collective-permute-done.15.refs_2_), channel_id=1, source_target_pairs={{0,1},{1,0},{2,3},{3,2},{4,5},{5,4},{6,7},{7,6},{8,9},{9,8},{10,11... | collective-permute-start | bytes 1572872 | tf_op jit(solution)/shard_map/ppermute | solution.py:22
  123.4 12.1 %collective-permute-start.29 = (bf16[2,4,2,32,512]{4,3,2,1,0:T(8,128)(2,1)S(1)}, bf16[2,4,2,32,512]{4,3,2,1,0:T(8,128)(2,1)}, u32[]{:S(2)}, u32[]{:S(2)}) collective-permute-start(bf16[2,4,2,32,512]{4,3,2,1,0:T(8,128)(2,1)S(1)} %collective-permute-done.16.refs_5_), channel_id=1, source_target_pairs={{0,1},{1,0},{2,3},{3,2},{4,5},{5,4},{6,7},{7,6},{8,9},{9,8},{10,11... | collective-permute-start | bytes 1572872 | tf_op jit(solution)/shard_map/ppermute | solution.py:22
  145.2 28.5 %collective-permute-start.37 = (bf16[64,4096]{1,0:T(8,128)(2,1)}, bf16[64,4096]{1,0:T(8,128)(2,1)S(1)}, u32[]{:S(2)}, u32[]{:S(2)}) collective-permute-start(bf16[64,4096]{1,0:T(8,128)(2,1)} %get-tuple-element.248), channel_id=1, source_target_pairs={{0,96},{32,0},{64,32},{96,64},{1,97},{33,1},{65,33},{97,65},{2,98}... | collective-permute-start | bytes 1572872 | tf_op jit(solution)/shard_map/ppermute | solution.py:18
  148.0 25.8 %collective-permute-start.38 = (bf16[64,4096]{1,0:T(8,128)(2,1)}, bf16[64,4096]{1,0:T(8,128)(2,1)S(1)}, u32[]{:S(2)}, u32[]{:S(2)}) collective-permute-start(bf16[64,4096]{1,0:T(8,128)(2,1)} %get-tuple-element.249), channel_id=1, source_target_pairs={{0,64},{32,96},{64,0},{96,32},{1,65},{33,97},{65,1},{97,33},{2,66}... | collective-permute-start | bytes 1572872 | tf_op jit(solution)/shard_map/ppermute | solution.py:18
  149.1 24.7 %collective-permute-start.39 = (bf16[64,4096]{1,0:T(8,128)(2,1)}, bf16[64,4096]{1,0:T(8,128)(2,1)S(1)}, u32[]{:S(2)}, u32[]{:S(2)}) collective-permute-start(bf16[64,4096]{1,0:T(8,128)(2,1)} %get-tuple-element.250), channel_id=1, source_target_pairs={{0,32},{32,64},{64,96},{96,0},{1,33},{33,65},{65,97},{97,1},{2,34}... | collective-permute-start | bytes 1572872 | tf_op jit(solution)/shard_map/ppermute | solution.py:18
  173.8 24.3 %all-to-all-start.4 = ((bf16[128,8,384]{2,1,0:T(8,128)(2,1)}), bf16[128,8,384]{2,1,0:T(8,128)(2,1)S(1)}, u32[]{:S(2)}, u32[]{:S(2)}) async-start(bf16[128,8,384]{2,1,0:T(8,128)(2,1)} %bitcast.18), calls=%async_computation.4 | async-start | bytes 1572864 | tf_op jit(solution)/shard_map/all_to_all | solution.py:678
  205.3 17.1 %collective-permute-start.41 = (bf16[32,4096]{1,0:T(8,128)(2,1)}, bf16[32,4096]{1,0:T(8,128)(2,1)S(1)}, u32[]{:S(2)}, u32[]{:S(2)}) collective-permute-start(bf16[32,4096]{1,0:T(8,128)(2,1)} %get-tuple-element.275), channel_id=1, source_target_pairs={{0,16},{16,0},{1,17},{17,1},{2,18},{18,2},{3,19},{19,3},{4,20},{20... | collective-permute-start | bytes 786440 | tf_op jit(solution)/shard_map/ppermute | solution.py:22
  210.2 13.0 %collective-permute-start.40 = (bf16[32,4096]{1,0:T(8,128)(2,1)}, bf16[32,4096]{1,0:T(8,128)(2,1)}, u32[]{:S(2)}, u32[]{:S(2)}) collective-permute-start(bf16[32,4096]{1,0:T(8,128)(2,1)} %get-tuple-element.273), channel_id=1, source_target_pairs={{0,2},{2,0},{1,3},{3,1},{4,6},{6,4},{5,7},{7,5},{8,10},{10,8},{9,1... | collective-permute-start | bytes 786440 | tf_op jit(solution)/shard_map/ppermute | solution.py:22
  216.5 34.3 %all-to-all-start.5 = ((bf16[64,32,512]{2,1,0:T(8,128)(2,1)}), bf16[64,32,512]{2,1,0:T(8,128)(2,1)S(1)}, u32[]{:S(2)}, u32[]{:S(2)}) async-start(bf16[64,32,512]{2,1,0:T(8,128)(2,1)} %shard_map.148), calls=%async_computation.5 | async-start | bytes 4194304 | tf_op jit(solution)/shard_map/all_to_all | solution.py:704
  (64 other events, 759.6 us)
where the time goes:
time: 254 us; the launch traced here: 252 us
  starting transfers between devices  85 us (33%)
  waiting for transfers between devices  73.2 us (29%)
  Pallas kernels  60.7 us (24%)
  local copies, waits for them, and re-layouts  17.4 us (7%)
  other arithmetic  14.5 us (6%)
    ppermute x25, starting transfers between devices, shift(): lax.ppermute(value, axis, [(i, (i + step) % size) for i in range(size)])  38.1 us
    all_to_all x1, waiting for transfers between devices, per_device(): arrived = lax.all_to_all(chip_sum, chips, 0, 0)  25.1 us
    ppermute x25, waiting for transfers between devices, shift(): lax.ppermute(value, axis, [(i, (i + step) % size) for i in range(size)])  18.6 us
    ppermute x26, waiting for transfers between devices, swap(): return lax.ppermute(value, axis, swap2)  17.2 us
    all_to_all x2, starting transfers between devices, spread(): lax.all_to_all(jnp.broadcast_to(block[None], (count,) + block.shape), axe...  13 us
    ppermute x26, starting transfers between devices, swap(): return lax.ppermute(value, axis, swap2)  12.8 us
    pallas_call x1, Pallas kernels, token_half(): pl.pallas_call(lambda *refs: token_kernel(n_seq, len(blocks), *refs), gri...  11.3 us
    pallas_call x1, Pallas kernels, down_parts(): pl.pallas_call(down_kernel, grid=(steps,), out_shape=[jax.ShapeDtypeStruc...  9.32 us
  transfers between devices with their start and end apart: 57, of which 20 were waited for; matrix products, arithmetic and copies ran while one was open for 9% of the time, Pallas kernels for 24%

commit v1 on v0

--- a/solution.py
+++ b/solution.py
@@ -696,9 +696,9 @@
         )
 
     up_block = trade(trade(up_block, "c", c_i), "yh", yh_i)
+    chip_sum, up_block = barrier((chip_sum, up_block))
     z_blocks = [lax.dynamic_index_in_dim(up_block, lax.rem(z_i + k, nz), 0, keepdims=False) for k in range(nz)]
     z_blocks = [z_blocks[0]] + [shift(z_blocks[k], "z", k, nz) for k in range(1, nz)]
-    chip_sum, z_blocks = barrier((chip_sum, z_blocks))
     query_grad = (q_own + swap(q_away, "yh").astype(f32)).astype(bf16)
     passage_grad = (p_own + swap(p_away, "yl").astype(f32)).astype(bf16)
     arrived = lax.all_to_all(chip_sum, chips, 0, 0)

time: 254 us -> 253 us (level)
  waiting for transfers between devices: 73.2 us -> 68 us
    all_to_all x1, waiting for transfers between devices: 25.1 us -> 9.49 us  [per_device(): arrived = lax.all_to_all(chip_sum, chips, 0, 0)]
    ppermute x25, waiting for transfers between devices: 18.6 us -> 29 us  [shift(): lax.ppermute(value, axis, [(i, (i + step) % size) for i in range(size)])]
  transfers between devices with their start and end apart: 57 -> 57, of which waited for: 20 -> 22; matrix products, arithmetic and copies ran while one was open for 9% -> 9% of each run, Pallas kernels for 24% -> 24%
where the time goes in v1:
time: 253 us; the launch traced here: 251 us
  starting transfers between devices  87.2 us (34%)
  waiting for transfers between devices  68 us (27%)
  Pallas kernels  60.7 us (24%)
  local copies, waits for them, and re-layouts  19.2 us (8%)
  other arithmetic  14.5 us (6%)
    ppermute x25, starting transfers between devices, shift(): lax.ppermute(value, axis, [(i, (i + step) % size) for i in range(size)])  39.6 us
    ppermute x25, waiting for transfers between devices, shift(): lax.ppermute(value, axis, [(i, (i + step) % size) for i in range(size)])  29 us
    ppermute x26, waiting for transfers between devices, swap(): return lax.ppermute(value, axis, swap2)  17.3 us
    all_to_all x2, starting transfers between devices, spread(): lax.all_to_all(jnp.broadcast_to(block[None], (count,) + block.shape), axe...  13 us
    ppermute x26, starting transfers between devices, swap(): return lax.ppermute(value, axis, swap2)  11.9 us
    pallas_call x1, Pallas kernels, token_half(): pl.pallas_call(lambda *refs: token_kernel(n_seq, len(blocks), *refs), gri...  11.3 us
    all_to_all x1, waiting for transfers between devices, per_device(): arrived = lax.all_to_all(chip_sum, chips, 0, 0)  9.49 us
    pallas_call x1, Pallas kernels, down_parts(): pl.pallas_call(down_kernel, grid=(steps,), out_shape=[jax.ShapeDtypeStruc...  9.32 us
  transfers between devices with their start and end apart: 57, of which 22 were waited for; matrix products, arithmetic and copies ran while one was open for 9% of the time, Pallas kernels for 24%

profile of v1, /device:TPU:0, one launch (start us, length us, event | category | flops | bytes accessed | tf_op | source)
XLA Modules:
  0.0 251.2 jit_solution(2445603137461967589)
XLA Ops:
  0.7 3.4 %collective-permute-start = (bf16[32,4096]{1,0:T(8,128)(2,1)}, bf16[32,4096]{1,0:T(8,128)(2,1)S(1)}, u32[]{:S(2)}, u32[]{:S(2)}) collective-permute-start(bf16[32,4096]{1,0:T(8,128)(2,1)} %bitcast.68), channel_id=1, source_target_pairs={{0,2},{2,0},{1,3},{3,1},{4,6},{6,4},{5,7},{7,5},{8,10},{10,8},{9,1... | collective-permute-start | bytes 786440 | tf_op jit(solution)/shard_map/ppermute | solution.py:22
  6.2 5.5 %collective-permute-done = bf16[32,4096]{1,0:T(8,128)(2,1)S(1)} collective-permute-done((bf16[32,4096]{1,0:T(8,128)(2,1)}, bf16[32,4096]{1,0:T(8,128)(2,1)S(1)}, u32[]{:S(2)}, u32[]{:S(2)}) %collective-permute-start) | collective-permute-done | bytes 262176 | tf_op jit(solution)/shard_map/ppermute | solution.py:22
  11.6 4.9 %collective-permute-done.1 = bf16[32,4096]{1,0:T(8,128)(2,1)S(1)} collective-permute-done((bf16[32,4096]{1,0:T(8,128)(2,1)}, bf16[32,4096]{1,0:T(8,128)(2,1)S(1)}, u32[]{:S(2)}, u32[]{:S(2)}) %collective-permute-start.1) | collective-permute-done | bytes 262176 | tf_op jit(solution)/shard_map/ppermute | solution.py:22
  26.3 5.3 %collective-permute-done.6.refs_6_.refs_10_.refs_2_ = bf16[64,4096]{1,0:T(8,128)(2,1)S(1)} collective-permute-done((bf16[64,4096]{1,0:T(8,128)(2,1)S(1)}, bf16[64,4096]{1,0:T(8,128)(2,1)S(1)}, u32[]{:S(2)}, u32[]{:S(2)}) %collective-permute-start.6) | collective-permute-done | bytes 524320 | tf_op jit(solution)/shard_map/ppermute | solution.py:18
  33.5 3.0 %collective-permute-start.9 = (bf16[32,4096]{1,0:T(8,128)(2,1)}, bf16[32,4096]{1,0:T(8,128)(2,1)}, u32[]{:S(2)}, u32[]{:S(2)}) collective-permute-start(bf16[32,4096]{1,0:T(8,128)(2,1)} %slice.91), channel_id=1, source_target_pairs={{0,96},{32,0},{64,32},{96,64},{1,97},{33,1},{65,33},{97,65},{2,98}... | collective-permute-start | bytes 786440 | tf_op jit(solution)/shard_map/ppermute | solution.py:18
  48.6 6.3 %all-to-all-start = ((bf16[16,64,512]{2,1,0:T(8,128)(2,1)}), bf16[16,64,512]{2,1,0:T(8,128)(2,1)}, u32[]{:S(2)}, u32[]{:S(2)}) async-start(bf16[16,64,512]{2,1,0:T(8,128)(2,1)} %broadcast_in_dim.139), calls=%async_computation | async-start | bytes 2097152 | tf_op jit(solution)/shard_map/all_to_all | solution.py:529
  60.2 5.1 %shard_map.137 = (f32[256,512]{1,0:T(8,128)}, f32[256,1]{1,0:T(8,128)}, f32[256,1]{1,0:T(8,128)}) custom-call(bf16[64,4096]{1,0:T(8,128)(2,1)} %copy-done.6, bf16[64,4096]{1,0:T(8,128)(2,1)} %copy-done.7, bf16[32,4096]{1,0:T(8,128)(2,1)} %collective-permute-done.3.refs_2_.refs_6_.refs_3_, bf16[32,4096]{1,0:T(8,128)(2,1)} %collective-permute-done.5.refs_3_.refs_7_.refs_4_, ...), custom_call_target="tpu_custom_call" | custom-call | tf_op jit(solution)/shard_map/pallas_call | solution.py:112
  69.5 3.2 %collective-permute-start.16 = (bf16[2,4,2,32,512]{4,3,2,1,0:T(8,128)(2,1)S(1)}, bf16[2,4,2,32,512]{4,3,2,1,0:T(8,128)(2,1)S(1)}, u32[]{:S(2)}, u32[]{:S(2)}) collective-permute-start(bf16[2,4,2,32,512]{4,3,2,1,0:T(8,128)(2,1)S(1)} %get-tuple-element.230.refs_1_), channel_id=1, source_target_pairs={{0,96},{32,0},{64,32},{96,64},{1,97},{33,1},{65,33},{97,65},{2,98}... | collective-permute-start | bytes 1572872 | tf_op jit(solution)/shard_map/ppermute | solution.py:18
  73.5 6.7 %all-to-all-start.1 = ((f32[8,1,640]{2,1,0:T(1,128)}), f32[8,1,640]{2,1,0:T(1,128)S(1)}, u32[]{:S(2)}, u32[]{:S(2)}) async-start(f32[8,1,640]{2,1,0:T(1,128)} %broadcast_in_dim.140), calls=%async_computation.1 | async-start | bytes 40960 | tf_op jit(solution)/shard_map/all_to_all | solution.py:529
  80.9 3.2 %collective-permute-start.18 = (bf16[2,4,2,32,512]{4,3,2,1,0:T(8,128)(2,1)S(1)}, bf16[2,4,2,32,512]{4,3,2,1,0:T(8,128)(2,1)S(1)}, u32[]{:S(2)}, u32[]{:S(2)}) collective-permute-start(bf16[2,4,2,32,512]{4,3,2,1,0:T(8,128)(2,1)S(1)} %get-tuple-element.224.refs_1_), channel_id=1, source_target_pairs={{0,96},{32,0},{64,32},{96,64},{1,97},{33,1},{65,33},{97,65},{2,98}... | collective-permute-start | bytes 1572872 | tf_op jit(solution)/shard_map/ppermute | solution.py:18
  84.1 3.7 %all-to-all-done.1 = f32[8,1,640]{2,1,0:T(1,128)S(1)} async-done(((f32[8,1,640]{2,1,0:T(1,128)}), f32[8,1,640]{2,1,0:T(1,128)S(1)}, u32[]{:S(2)}, u32[]{:S(2)}) %all-to-all-start.1) | async-done | bytes 20512 | tf_op jit(solution)/shard_map/all_to_all | solution.py:529
  89.3 6.3 %shard_map.138 = (bf16[256,512]{1,0:T(8,128)(2,1)}, bf16[8,4,4096]{2,1,0:T(4,128)(2,1)}, bf16[16,2,4096]{2,1,0:T(2,128)(2,1)}) custom-call(s32[17]{0:T(128)} %concatenate.40.refs_0_.core, f32[256,512]{1,0:T(8,128)} %get-tuple-element.174.refs_1_, f32[256,3]{1,0:T(8,128)} %copy.42.refs_2_, s32[1,512]{1,0:T(1,128)} %add.343.refs_3_, ...), custom_call_target="tpu_custom_call" | custom-call | tf_op jit(solution)/shard_map/pallas_call | solution.py:167
  95.7 3.8 %all-to-all-start.2 = ((bf16[8,4,4096]{2,1,0:T(4,128)(2,1)}), bf16[8,4,4096]{2,1,0:T(4,128)(2,1)S(1)}, u32[]{:S(2)}, u32[]{:S(2)}) async-start(bf16[8,4,4096]{2,1,0:T(4,128)(2,1)} %get-tuple-element.183), calls=%async_computation.2 | async-start | bytes 524288 | tf_op jit(solution)/shard_map/all_to_all | solution.py:634
  100.2 4.4 %shard_map.139 = (bf16[64,4096]{1,0:T(8,128)(2,1)}, bf16[64,4096]{1,0:T(8,128)(2,1)}, bf16[64,4096]{1,0:T(8,128)(2,1)}, bf16[64,4096]{1,0:T(8,128)(2,1)}) custom-call(bf16[256,512]{1,0:T(8,128)(2,1)} %get-tuple-element.190.refs_0_, bf16[64,4096]{1,0:T(8,128)(2,1)} %copy-done, bf16[64,4096]{1,0:T(8,128)(2,1)} %copy-done.1, bf16[32,4096]{1,0:T(8,128)(2,1)} %copy-done.8, ...), custom_call_target="tpu_custom_call" | custom-call | flops 1073741824 | bytes 6291456 | tf_op jit(solution)/shard_map/pallas_call | solution.py:283
  104.6 3.6 %all-to-all-done.2 = bf16[8,4,4096]{2,1,0:T(4,128)(2,1)S(1)} async-done(((bf16[8,4,4096]{2,1,0:T(4,128)(2,1)}), bf16[8,4,4096]{2,1,0:T(4,128)(2,1)S(1)}, u32[]{:S(2)}, u32[]{:S(2)}) %all-to-all-start.2) | async-done | bytes 262176 | tf_op jit(solution)/shard_map/all_to_all | solution.py:634
  111.5 3.0 %collective-permute-start.20 = (bf16[1,4,2,32,512]{4,3,2,1,0:T(8,128)(2,1)}, bf16[1,4,2,32,512]{4,3,2,1,0:T(8,128)(2,1)S(1)}, u32[]{:S(2)}, u32[]{:S(2)}) collective-permute-start(bf16[1,4,2,32,512]{4,3,2,1,0:T(8,128)(2,1)} %slice.77), channel_id=1, source_target_pairs={{0,96},{32,0},{64,32},{96,64},{1,97},{33,1},{65,33},{97,65},{2,98}... | collective-permute-start | bytes 786440 | tf_op jit(solution)/shard_map/ppermute | solution.py:18
  114.4 3.5 %all-to-all-start.3 = ((bf16[16,2,4096]{2,1,0:T(2,128)(2,1)}), bf16[16,2,4096]{2,1,0:T(2,128)(2,1)S(1)}, u32[]{:S(2)}, u32[]{:S(2)}) async-start(bf16[16,2,4096]{2,1,0:T(2,128)(2,1)} %get-tuple-element.189), calls=%async_computation.3 | async-start | bytes 524288 | tf_op jit(solution)/shard_map/all_to_all | solution.py:633
  118.0 4.2 %shard_map.140 = (bf16[64,4096]{1,0:T(8,128)(2,1)}, bf16[64,4096]{1,0:T(8,128)(2,1)}, bf16[64,4096]{1,0:T(8,128)(2,1)}, bf16[64,4096]{1,0:T(8,128)(2,1)}, bf16[6...) custom-call(bf16[256,512]{1,0:T(8,128)(2,1)} %get-tuple-element.190.refs_0_,, ...), custom_call_target="tpu_custom_call" | custom-call | flops 1073741824 | bytes 6291456 | tf_op jit(solution)/shard_map/pallas_call | solution.py:283
  125.8 7.5 %collective-permute-done.23.refs_3_ = bf16[64,4096]{1,0:T(8,128)(2,1)} collective-permute-done((bf16[64,4096]{1,0:T(8,128)(2,1)}, bf16[64,4096]{1,0:T(8,128)(2,1)}, u32[]{:S(2)}, u32[]{:S(2)}) %collective-permute-start.23) | collective-permute-done | bytes 524320 | tf_op jit(solution)/shard_map/ppermute | solution.py:18
  140.1 3.3 %shard_map.141 = (bf16[64,4096]{1,0:T(8,128)(2,1)}, bf16[64,4096]{1,0:T(8,128)(2,1)}, bf16[64,4096]{1,0:T(8,128)(2,1)}, bf16[64,4096]{1,0:T(8,128)(2,1)}) custom-call(bf16[64,4096]{1,0:T(8,128)(2,1)} %get-tuple-element.210.refs_0_, bf16[64,4096]{1,0:T(8,128)(2,1)} %get-tuple-element.211.refs_1_, bf16[64,4096]{1,0:T(8,128)(2,1)} %get-tuple-element.212.refs_2_, ...), custom_call_target="tpu_custom_call" | custom-call | tf_op jit(solution)/shard_map/pallas_call | solution.py:223
  145.2 2.8 %collective-permute-start.37 = (bf16[64,4096]{1,0:T(8,128)(2,1)}, bf16[64,4096]{1,0:T(8,128)(2,1)S(1)}, u32[]{:S(2)}, u32[]{:S(2)}) collective-permute-start(bf16[64,4096]{1,0:T(8,128)(2,1)} %get-tuple-element.245), channel_id=1, source_target_pairs={{0,96},{32,0},{64,32},{96,64},{1,97},{33,1},{65,33},{97,65},{2,98}... | collective-permute-start | bytes 1572872 | tf_op jit(solution)/shard_map/ppermute | solution.py:18
  149.8 11.3 %shard_map.143 = (f32[128,512]{1,0:T(8,128)}, f32[768,512]{1,0:T(8,128)}, f32[8,512]{1,0:T(8,128)}) custom-call(s32[17]{0:T(128)} %concatenate.40.refs_0_.core, bf16[2,4,2,32,512]{4,3,2,1,0:T(8,128)(2,1)} %copy-done.12, bf16[2,4,2,32,512]{4,3,2,1,0:T(8,128)(2,1)} %copy-done.13, bf16[1,4,2,32,512]{4,3,2,1,0:T(8,128)(2,1)} %collective-permute-done.19.refs_3_, ...), custom_call_target="tpu_custom_call" | custom-call | tf_op jit(solution)/shard_map/pallas_call | solution.py:425
  161.9 4.5 %shard_map.142 = f32[16,256]{1,0:T(8,128)} custom-call(bf16[16,4096]{1,0:T(8,128)(2,1)} %pad_maximum_fusion.3.refs_0_, bf16[2,4,2,32,512]{4,3,2,1,0:T(8,128)(2,1)} %copy-done.11, bf16[2,4,2,32,512]{4,3,2,1,0:T(8,128)(2,1)} %copy-done.15, bf16[1,4,2,32,512]{4,3,2,1,0:T(8,128)(2,1)} %copy-done.29, bf16[1,4,2,32,512]{4,3,2,1,0:T(8,128)(2,1)} %copy-done.30, ...), custom_call_target="tpu_custom_call" | custom-call | tf_op jit(solution)/shard_map/pallas_call | solution.py:486
  169.5 4.2 %shard_map.144 = (bf16[128,512]{1,0:T(8,128)(2,1)}, bf16[768,512]{1,0:T(8,128)(2,1)}) custom-call(s32[17]{0:T(128)} %concatenate.40.refs_0_.core, f32[8,256]{1,0:T(8,128)} %get-tuple-element.304.refs_1_, f32[8,256]{1,0:T(8,128)} %copy-done.35, bf16[512,512]{1,0:T(8,128)(2,1)} %fusion.refs_3_, f32[128,512]{1,0:T(8,128)} %get-tuple-element.240.refs_4_, ...), custom_call_target="tpu_custom_call" | custom-call | tf_op jit(solution)/shard_map/pallas_call | solution.py:518
  173.8 7.9 %all-to-all-start.4 = ((bf16[128,8,384]{2,1,0:T(8,128)(2,1)}), bf16[128,8,384]{2,1,0:T(8,128)(2,1)S(1)}, u32[]{:S(2)}, u32[]{:S(2)}) async-start(bf16[128,8,384]{2,1,0:T(8,128)(2,1)} %bitcast.18), calls=%async_computation.4 | async-start | bytes 1572864 | tf_op jit(solution)/shard_map/all_to_all | solution.py:678
  186.4 9.3 %shard_map.145 = (bf16[64,32,512]{2,1,0:T(8,128)(2,1)}, bf16[16,32,512]{2,1,0:T(8,128)(2,1)}, bf16[16,32,512]{2,1,0:T(8,128)(2,1)}, bf16[16,32,512]{2,1,0:T(8,128)(2,1)}, bf16[16,32,512]{2,1,0:T(8,128)(2,1)}) custom-call(s32[17]{0:T(128)} %concatenate.40.refs_0_.core, bf16[128,4096]{1,0:T(8,128)(2,1)} %bitcast.64, bf16[768,4096]{1,0:T(8,128)(2,1)} %bitcast.61, ...), custom_call_target="tpu_custom_call" | custom-call | flops 3758096384 | bytes 8388608 | tf_op jit(solution)/shard_map/pallas_call | solution.py:337
  200.9 4.4 %collective-permute-done.47 = f32[4,4,2,256]{3,2,1,0:T(2,128)S(1)} collective-permute-done((f32[4,4,2,256]{3,2,1,0:T(2,128)S(1)}, f32[4,4,2,256]{3,2,1,0:T(2,128)S(1)}, u32[]{:S(2)}, u32[]{:S(2)}) %collective-permute-start.47) | collective-permute-done | bytes 32800 | tf_op jit(solution)/shard_map/ppermute | solution.py:22
  209.8 3.4 %shard_map.148 = bf16[64,32,512]{2,1,0:T(8,128)(2,1)} custom-call(bf16[64,32,512]{2,1,0:T(8,128)(2,1)} %get-tuple-element.273.refs_0_, bf16[16,32,512]{2,1,0:T(8,128)(2,1)} %copy-done.17, bf16[16,32,512]{2,1,0:T(8,128)(2,1)} %copy-done.18, bf16[16,32,512]{2,1,0:T(8,128)(2,1)} %copy-done.19, bf16[16,32,512]{2,1,0:T(8,128)(2,1)} %copy-done.20), custom_call_target="tpu_custom_call" | custom-call | tf_op jit(solution)/shard_map/pallas_call | solution.py:249
  213.2 7.4 %all-to-all-start.5 = ((bf16[64,32,512]{2,1,0:T(8,128)(2,1)}), bf16[64,32,512]{2,1,0:T(8,128)(2,1)S(1)}, u32[]{:S(2)}, u32[]{:S(2)}) async-start(bf16[64,32,512]{2,1,0:T(8,128)(2,1)} %shard_map.148), calls=%async_computation.5 | async-start | bytes 4194304 | tf_op jit(solution)/shard_map/all_to_all | solution.py:704
  224.7 2.7 %collective-permute-start.49 = (f32[4,4,256]{2,1,0:T(4,128)S(1)}, f32[4,4,256]{2,1,0:T(4,128)S(1)}, u32[]{:S(2)}, u32[]{:S(2)}) collective-permute-start(f32[4,4,256]{2,1,0:T(4,128)S(1)} %get-tuple-element.295), channel_id=1, source_target_pairs={{0,8},{4,12},{8,0},{12,4},{1,9},{5,13},{9,1},{13,5},{2,10},{6,14},... | collective-permute-start | bytes 49160 | tf_op jit(solution)/shard_map/ppermute | solution.py:18
  230.2 9.1 %collective-permute-done.49 = f32[4,4,256]{2,1,0:T(4,128)S(1)} collective-permute-done((f32[4,4,256]{2,1,0:T(4,128)S(1)}, f32[4,4,256]{2,1,0:T(4,128)S(1)}, u32[]{:S(2)}, u32[]{:S(2)}) %collective-permute-start.49) | collective-permute-done | bytes 16416 | tf_op jit(solution)/shard_map/ppermute | solution.py:18
  240.1 9.5 %all-to-all-done.5 = bf16[64,32,512]{2,1,0:T(8,128)(2,1)S(1)} async-done(((bf16[64,32,512]{2,1,0:T(8,128)(2,1)}), bf16[64,32,512]{2,1,0:T(8,128)(2,1)S(1)}, u32[]{:S(2)}, u32[]{:S(2)}) %all-to-all-start.5) | async-done | bytes 2097184 | tf_op jit(solution)/shard_map/all_to_all | solution.py:704
  (257 shorter events, 83.5 us)
Async XLA Ops:
  4.0 12.5 %collective-permute-start.1 = (bf16[32,4096]{1,0:T(8,128)(2,1)}, bf16[32,4096]{1,0:T(8,128)(2,1)S(1)}, u32[]{:S(2)}, u32[]{:S(2)}) collective-permute-start(bf16[32,4096]{1,0:T(8,128)(2,1)} %bitcast.66), channel_id=1, source_target_pairs={{0,16},{16,0},{1,17},{17,1},{2,18},{18,2},{3,19},{19,3},{4,20},{20... | collective-permute-start | bytes 786440 | tf_op jit(solution)/shard_map/ppermute | solution.py:22
  17.5 14.1 %collective-permute-start.6 = (bf16[64,4096]{1,0:T(8,128)(2,1)S(1)}, bf16[64,4096]{1,0:T(8,128)(2,1)S(1)}, u32[]{:S(2)}, u32[]{:S(2)}) collective-permute-start(bf16[64,4096]{1,0:T(8,128)(2,1)S(1)} %pad_maximum_fusion.2.refs_5_.refs_9_.refs_1_), channel_id=1, source_target_pairs={{0,32},{32,64},{64,96},{96,0},{1,33},{33,65},{65,97},{97,1},{2,34}... | collective-permute-start | bytes 1572872 | tf_op jit(solution)/shard_map/ppermute | solution.py:18
  19.1 13.6 %collective-permute-start.8 = (bf16[64,4096]{1,0:T(8,128)(2,1)S(1)}, bf16[64,4096]{1,0:T(8,128)(2,1)S(1)}, u32[]{:S(2)}, u32[]{:S(2)}) collective-permute-start(bf16[64,4096]{1,0:T(8,128)(2,1)S(1)} %pad_maximum_fusion.2.refs_5_.refs_9_.refs_1_), channel_id=1, source_target_pairs={{0,96},{32,0},{64,32},{96,64},{1,97},{33,1},{65,33},{97,65},{2,98}... | collective-permute-start | bytes 1572872 | tf_op jit(solution)/shard_map/ppermute | solution.py:18
  21.8 14.6 %collective-permute-start.2 = (bf16[64,4096]{1,0:T(8,128)(2,1)S(1)}, bf16[64,4096]{1,0:T(8,128)(2,1)S(1)}, u32[]{:S(2)}, u32[]{:S(2)}) collective-permute-start(bf16[64,4096]{1,0:T(8,128)(2,1)S(1)} %pad_maximum_fusion.1.refs_0_.refs_4_.refs_1_), channel_id=1, source_target_pairs={{0,4},{4,8},{8,12},{12,0},{1,5},{5,9},{9,13},{13,1},{2,6},{6,10},{... | collective-permute-start | bytes 1572872 | tf_op jit(solution)/shard_map/ppermute | solution.py:18
  23.8 15.3 %collective-permute-start.4 = (bf16[64,4096]{1,0:T(8,128)(2,1)S(1)}, bf16[64,4096]{1,0:T(8,128)(2,1)}, u32[]{:S(2)}, u32[]{:S(2)}) collective-permute-start(bf16[64,4096]{1,0:T(8,128)(2,1)S(1)} %pad_maximum_fusion.1.refs_0_.refs_4_.refs_1_), channel_id=1, source_target_pairs={{0,12},{4,0},{8,4},{12,8},{1,13},{5,1},{9,5},{13,9},{2,14},{6,2},{... | collective-permute-start | bytes 1572872 | tf_op jit(solution)/shard_map/ppermute | solution.py:18
  26.0 18.5 %collective-permute-start.10 = (bf16[64,4096]{1,0:T(8,128)(2,1)S(1)}, bf16[64,4096]{1,0:T(8,128)(2,1)S(1)}, u32[]{:S(2)}, u32[]{:S(2)}) collective-permute-start(bf16[64,4096]{1,0:T(8,128)(2,1)S(1)} %pad_maximum_fusion.2.refs_5_.refs_9_.refs_1_), channel_id=1, source_target_pairs={{0,1},{1,0},{2,3},{3,2},{4,5},{5,4},{6,7},{7,6},{8,9},{9,8},{10,11... | collective-permute-start | bytes 1572872 | tf_op jit(solution)/shard_map/ppermute | solution.py:22
  32.4 12.1 %collective-permute-start.7 = (bf16[32,4096]{1,0:T(8,128)(2,1)}, bf16[32,4096]{1,0:T(8,128)(2,1)S(1)}, u32[]{:S(2)}, u32[]{:S(2)}) collective-permute-start(bf16[32,4096]{1,0:T(8,128)(2,1)} %slice.90), channel_id=1, source_target_pairs={{0,32},{32,64},{64,96},{96,0},{1,33},{33,65},{65,97},{97,1},{2,34}... | collective-permute-start | bytes 786440 | tf_op jit(solution)/shard_map/ppermute | solution.py:18
  33.5 11.1 %collective-permute-start.9 = (bf16[32,4096]{1,0:T(8,128)(2,1)}, bf16[32,4096]{1,0:T(8,128)(2,1)}, u32[]{:S(2)}, u32[]{:S(2)}) collective-permute-start(bf16[32,4096]{1,0:T(8,128)(2,1)} %slice.91), channel_id=1, source_target_pairs={{0,96},{32,0},{64,32},{96,64},{1,97},{33,1},{65,33},{97,65},{2,98}... | collective-permute-start | bytes 786440 | tf_op jit(solution)/shard_map/ppermute | solution.py:18
  48.6 19.5 %all-to-all-start = ((bf16[16,64,512]{2,1,0:T(8,128)(2,1)}), bf16[16,64,512]{2,1,0:T(8,128)(2,1)}, u32[]{:S(2)}, u32[]{:S(2)}) async-start(bf16[16,64,512]{2,1,0:T(8,128)(2,1)} %broadcast_in_dim.139), calls=%async_computation | async-start | bytes 2097152 | tf_op jit(solution)/shard_map/all_to_all | solution.py:529
  69.4 18.5 %collective-permute-start.15 = (bf16[2,4,2,32,512]{4,3,2,1,0:T(8,128)(2,1)S(1)}, bf16[2,4,2,32,512]{4,3,2,1,0:T(8,128)(2,1)S(1)}, u32[]{:S(2)}, u32[]{:S(2)}) collective-permute-start(bf16[2,4,2,32,512]{4,3,2,1,0:T(8,128)(2,1)S(1)} %get-tuple-element.230.refs_1_), channel_id=1, source_target_pairs={{0,32},{32,64},{64,96},{96,0},{1,33},{33,65},{65,97},{97,1},{2,34}... | collective-permute-start | bytes 1572872 | tf_op jit(solution)/shard_map/ppermute | solution.py:18
  69.5 18.4 %collective-permute-start.16 = (bf16[2,4,2,32,512]{4,3,2,1,0:T(8,128)(2,1)S(1)}, bf16[2,4,2,32,512]{4,3,2,1,0:T(8,128)(2,1)S(1)}, u32[]{:S(2)}, u32[]{:S(2)}) collective-permute-start(bf16[2,4,2,32,512]{4,3,2,1,0:T(8,128)(2,1)S(1)} %get-tuple-element.230.refs_1_), channel_id=1, source_target_pairs={{0,96},{32,0},{64,32},{96,64},{1,97},{33,1},{65,33},{97,65},{2,98}... | collective-permute-start | bytes 1572872 | tf_op jit(solution)/shard_map/ppermute | solution.py:18
  73.5 14.4 %all-to-all-start.1 = ((f32[8,1,640]{2,1,0:T(1,128)}), f32[8,1,640]{2,1,0:T(1,128)S(1)}, u32[]{:S(2)}, u32[]{:S(2)}) async-start(f32[8,1,640]{2,1,0:T(1,128)} %broadcast_in_dim.140), calls=%async_computation.1 | async-start | bytes 40960 | tf_op jit(solution)/shard_map/all_to_all | solution.py:529
  80.9 23.7 %collective-permute-start.17 = (bf16[2,4,2,32,512]{4,3,2,1,0:T(8,128)(2,1)S(1)}, bf16[2,4,2,32,512]{4,3,2,1,0:T(8,128)(2,1)S(1)}, u32[]{:S(2)}, u32[]{:S(2)}) collective-permute-start(bf16[2,4,2,32,512]{4,3,2,1,0:T(8,128)(2,1)S(1)} %get-tuple-element.224.refs_1_), channel_id=1, source_target_pairs={{0,32},{32,64},{64,96},{96,0},{1,33},{33,65},{65,97},{97,1},{2,34}... | collective-permute-start | bytes 1572872 | tf_op jit(solution)/shard_map/ppermute | solution.py:18
  80.9 23.7 %collective-permute-start.18 = (bf16[2,4,2,32,512]{4,3,2,1,0:T(8,128)(2,1)S(1)}, bf16[2,4,2,32,512]{4,3,2,1,0:T(8,128)(2,1)S(1)}, u32[]{:S(2)}, u32[]{:S(2)}) collective-permute-start(bf16[2,4,2,32,512]{4,3,2,1,0:T(8,128)(2,1)S(1)} %get-tuple-element.224.refs_1_), channel_id=1, source_target_pairs={{0,96},{32,0},{64,32},{96,64},{1,97},{33,1},{65,33},{97,65},{2,98}... | collective-permute-start | bytes 1572872 | tf_op jit(solution)/shard_map/ppermute | solution.py:18
  95.7 12.5 %all-to-all-start.2 = ((bf16[8,4,4096]{2,1,0:T(4,128)(2,1)}), bf16[8,4,4096]{2,1,0:T(4,128)(2,1)S(1)}, u32[]{:S(2)}, u32[]{:S(2)}) async-start(bf16[8,4,4096]{2,1,0:T(4,128)(2,1)} %get-tuple-element.183), calls=%async_computation.2 | async-start | bytes 524288 | tf_op jit(solution)/shard_map/all_to_all | solution.py:634
  100.2 11.3 %collective-permute-start.19 = (bf16[1,4,2,32,512]{4,3,2,1,0:T(8,128)(2,1)}, bf16[1,4,2,32,512]{4,3,2,1,0:T(8,128)(2,1)}, u32[]{:S(2)}, u32[]{:S(2)}) collective-permute-start(bf16[1,4,2,32,512]{4,3,2,1,0:T(8,128)(2,1)} %slice.76), channel_id=1, source_target_pairs={{0,32},{32,64},{64,96},{96,0},{1,33},{33,65},{65,97},{97,1},{2,34}... | collective-permute-start | bytes 786440 | tf_op jit(solution)/shard_map/ppermute | solution.py:18
  108.2 15.2 %collective-permute-start.21 = (bf16[64,4096]{1,0:T(8,128)(2,1)}, bf16[64,4096]{1,0:T(8,128)(2,1)}, u32[]{:S(2)}, u32[]{:S(2)}) collective-permute-start(bf16[64,4096]{1,0:T(8,128)(2,1)} %get-tuple-element.204), channel_id=1, source_target_pairs={{0,12},{4,0},{8,4},{12,8},{1,13},{5,1},{9,5},{13,9},{2,14},{6,2},{... | collective-permute-start | bytes 1572872 | tf_op jit(solution)/shard_map/ppermute | solution.py:18
  109.1 16.7 %collective-permute-start.22 = (bf16[64,4096]{1,0:T(8,128)(2,1)}, bf16[64,4096]{1,0:T(8,128)(2,1)}, u32[]{:S(2)}, u32[]{:S(2)}) collective-permute-start(bf16[64,4096]{1,0:T(8,128)(2,1)} %get-tuple-element.205), channel_id=1, source_target_pairs={{0,8},{4,12},{8,0},{12,4},{1,9},{5,13},{9,1},{13,5},{2,10},{6,14},... | collective-permute-start | bytes 1572872 | tf_op jit(solution)/shard_map/ppermute | solution.py:18
  110.5 22.7 %collective-permute-start.23 = (bf16[64,4096]{1,0:T(8,128)(2,1)}, bf16[64,4096]{1,0:T(8,128)(2,1)}, u32[]{:S(2)}, u32[]{:S(2)}) collective-permute-start(bf16[64,4096]{1,0:T(8,128)(2,1)} %get-tuple-element.206), channel_id=1, source_target_pairs={{0,4},{4,8},{8,12},{12,0},{1,5},{5,9},{9,13},{13,1},{2,6},{6,10},{... | collective-permute-start | bytes 1572872 | tf_op jit(solution)/shard_map/ppermute | solution.py:18
  110.8 23.0 %collective-permute-start.25 = (bf16[2,4,2,32,512]{4,3,2,1,0:T(8,128)(2,1)S(1)}, bf16[2,4,2,32,512]{4,3,2,1,0:T(8,128)(2,1)}, u32[]{:S(2)}, u32[]{:S(2)}) collective-permute-start(bf16[2,4,2,32,512]{4,3,2,1,0:T(8,128)(2,1)S(1)} %get-tuple-element.230.refs_1_), channel_id=1, source_target_pairs={{0,1},{1,0},{2,3},{3,2},{4,5},{5,4},{6,7},{7,6},{8,9},{9,8},{10,11... | collective-permute-start | bytes 1572872 | tf_op jit(solution)/shard_map/ppermute | solution.py:22
  114.4 11.2 %all-to-all-start.3 = ((bf16[16,2,4096]{2,1,0:T(2,128)(2,1)}), bf16[16,2,4096]{2,1,0:T(2,128)(2,1)S(1)}, u32[]{:S(2)}, u32[]{:S(2)}) async-start(bf16[16,2,4096]{2,1,0:T(2,128)(2,1)} %get-tuple-element.189), calls=%async_computation.3 | async-start | bytes 524288 | tf_op jit(solution)/shard_map/all_to_all | solution.py:633
  122.4 12.5 %collective-permute-start.26 = (bf16[2,4,2,32,512]{4,3,2,1,0:T(8,128)(2,1)S(1)}, bf16[2,4,2,32,512]{4,3,2,1,0:T(8,128)(2,1)}, u32[]{:S(2)}, u32[]{:S(2)}) collective-permute-start(bf16[2,4,2,32,512]{4,3,2,1,0:T(8,128)(2,1)S(1)} %collective-permute-done.15.refs_2_), channel_id=1, source_target_pairs={{0,1},{1,0},{2,3},{3,2},{4,5},{5,4},{6,7},{7,6},{8,9},{9,8},{10,11... | collective-permute-start | bytes 1572872 | tf_op jit(solution)/shard_map/ppermute | solution.py:22
  123.4 12.1 %collective-permute-start.29 = (bf16[2,4,2,32,512]{4,3,2,1,0:T(8,128)(2,1)S(1)}, bf16[2,4,2,32,512]{4,3,2,1,0:T(8,128)(2,1)}, u32[]{:S(2)}, u32[]{:S(2)}) collective-permute-start(bf16[2,4,2,32,512]{4,3,2,1,0:T(8,128)(2,1)S(1)} %collective-permute-done.16.refs_5_), channel_id=1, source_target_pairs={{0,1},{1,0},{2,3},{3,2},{4,5},{5,4},{6,7},{7,6},{8,9},{9,8},{10,11... | collective-permute-start | bytes 1572872 | tf_op jit(solution)/shard_map/ppermute | solution.py:22
  145.2 28.5 %collective-permute-start.37 = (bf16[64,4096]{1,0:T(8,128)(2,1)}, bf16[64,4096]{1,0:T(8,128)(2,1)S(1)}, u32[]{:S(2)}, u32[]{:S(2)}) collective-permute-start(bf16[64,4096]{1,0:T(8,128)(2,1)} %get-tuple-element.245), channel_id=1, source_target_pairs={{0,96},{32,0},{64,32},{96,64},{1,97},{33,1},{65,33},{97,65},{2,98}... | collective-permute-start | bytes 1572872 | tf_op jit(solution)/shard_map/ppermute | solution.py:18
  148.0 25.8 %collective-permute-start.38 = (bf16[64,4096]{1,0:T(8,128)(2,1)}, bf16[64,4096]{1,0:T(8,128)(2,1)S(1)}, u32[]{:S(2)}, u32[]{:S(2)}) collective-permute-start(bf16[64,4096]{1,0:T(8,128)(2,1)} %get-tuple-element.246), channel_id=1, source_target_pairs={{0,64},{32,96},{64,0},{96,32},{1,65},{33,97},{65,1},{97,33},{2,66}... | collective-permute-start | bytes 1572872 | tf_op jit(solution)/shard_map/ppermute | solution.py:18
  149.1 24.7 %collective-permute-start.39 = (bf16[64,4096]{1,0:T(8,128)(2,1)}, bf16[64,4096]{1,0:T(8,128)(2,1)S(1)}, u32[]{:S(2)}, u32[]{:S(2)}) collective-permute-start(bf16[64,4096]{1,0:T(8,128)(2,1)} %get-tuple-element.247), channel_id=1, source_target_pairs={{0,32},{32,64},{64,96},{96,0},{1,33},{33,65},{65,97},{97,1},{2,34}... | collective-permute-start | bytes 1572872 | tf_op jit(solution)/shard_map/ppermute | solution.py:18
  173.8 24.3 %all-to-all-start.4 = ((bf16[128,8,384]{2,1,0:T(8,128)(2,1)}), bf16[128,8,384]{2,1,0:T(8,128)(2,1)S(1)}, u32[]{:S(2)}, u32[]{:S(2)}) async-start(bf16[128,8,384]{2,1,0:T(8,128)(2,1)} %bitcast.18), calls=%async_computation.4 | async-start | bytes 1572864 | tf_op jit(solution)/shard_map/all_to_all | solution.py:678
  205.3 15.4 %collective-permute-start.41 = (bf16[32,4096]{1,0:T(8,128)(2,1)}, bf16[32,4096]{1,0:T(8,128)(2,1)S(1)}, u32[]{:S(2)}, u32[]{:S(2)}) collective-permute-start(bf16[32,4096]{1,0:T(8,128)(2,1)} %get-tuple-element.272), channel_id=1, source_target_pairs={{0,16},{16,0},{1,17},{17,1},{2,18},{18,2},{3,19},{19,3},{4,20},{20... | collective-permute-start | bytes 786440 | tf_op jit(solution)/shard_map/ppermute | solution.py:22
  206.0 15.4 %collective-permute-start.40 = (bf16[32,4096]{1,0:T(8,128)(2,1)}, bf16[32,4096]{1,0:T(8,128)(2,1)}, u32[]{:S(2)}, u32[]{:S(2)}) collective-permute-start(bf16[32,4096]{1,0:T(8,128)(2,1)} %get-tuple-element.270), channel_id=1, source_target_pairs={{0,2},{2,0},{1,3},{3,1},{4,6},{6,4},{5,7},{7,5},{8,10},{10,8},{9,1... | collective-permute-start | bytes 786440 | tf_op jit(solution)/shard_map/ppermute | solution.py:22
  213.2 36.3 %all-to-all-start.5 = ((bf16[64,32,512]{2,1,0:T(8,128)(2,1)}), bf16[64,32,512]{2,1,0:T(8,128)(2,1)S(1)}, u32[]{:S(2)}, u32[]{:S(2)}) async-start(bf16[64,32,512]{2,1,0:T(8,128)(2,1)} %shard_map.148), calls=%async_computation.5 | async-start | bytes 4194304 | tf_op jit(solution)/shard_map/all_to_all | solution.py:704
  224.7 14.6 %collective-permute-start.49 = (f32[4,4,256]{2,1,0:T(4,128)S(1)}, f32[4,4,256]{2,1,0:T(4,128)S(1)}, u32[]{:S(2)}, u32[]{:S(2)}) collective-permute-start(f32[4,4,256]{2,1,0:T(4,128)S(1)} %get-tuple-element.295), channel_id=1, source_target_pairs={{0,8},{4,12},{8,0},{12,4},{1,9},{5,13},{9,1},{13,5},{2,10},{6,14},... | collective-permute-start | bytes 49160 | tf_op jit(solution)/shard_map/ppermute | solution.py:18
  227.4 12.0 %collective-permute-start.50 = (f32[4,4,256]{2,1,0:T(4,128)S(1)}, f32[4,4,256]{2,1,0:T(4,128)S(1)}, u32[]{:S(2)}, u32[]{:S(2)}) collective-permute-start(f32[4,4,256]{2,1,0:T(4,128)S(1)} %get-tuple-element.294), channel_id=1, source_target_pairs={{0,12},{4,0},{8,4},{12,8},{1,13},{5,1},{9,5},{13,9},{2,14},{6,2},{... | collective-permute-start | bytes 49160 | tf_op jit(solution)/shard_map/ppermute | solution.py:18
  (64 other events, 747.2 us)

commit v2 on v1

--- a/solution.py
+++ b/solution.py
@@ -180,32 +180,36 @@
 
 
 def ring_add_kernel(n, *refs):
-    total = refs[0][...].astype(f32)
-    for r in refs[1:n]:
-        total = total + r[...].astype(f32)
-    half = total.shape[0] // 2
-    refs[n][...] = total[:half]
-    refs[n + 1][...] = total[half:].astype(bf16)
-
-
-def ring_add(terms):
-    rows, width = terms[0].shape
-    tile = width // 2
+    for k in range(2):
+        terms, out = refs[k * n : (k + 1) * n], refs[2 * n + 2 * k : 2 * n + 2 * k + 2]
+        total = terms[0][...].astype(f32)
+        for r in terms[1:]:
+            total = total + r[...].astype(f32)
+        half = total.shape[0] // 2
+        out[0][...] = total[:half]
+        out[1][...] = total[half:].astype(bf16)
+
+
+def ring_add(first, second):
+    rows, width = first[0].shape
+    n = len(first)
+    tile = width // 4
 
     def cut(n):
         return pl.BlockSpec((n, tile), lambda i: (0, i))
 
-    return pl.pallas_call(
-        lambda *refs: ring_add_kernel(len(terms), *refs),
-        grid=(2,),
-        out_shape=(jax.ShapeDtypeStruct((rows // 2, width), f32), jax.ShapeDtypeStruct((rows // 2, width), bf16)),
-        in_specs=[cut(rows)] * len(terms),
-        out_specs=(cut(rows // 2),) * 2,
+    half = [jax.ShapeDtypeStruct((rows // 2, width), f32), jax.ShapeDtypeStruct((rows // 2, width), bf16)]
+    return pl.pallas_call(
+        lambda *refs: ring_add_kernel(n, *refs),
+        grid=(4,),
+        out_shape=half * 2,
+        in_specs=[cut(rows)] * (2 * n),
+        out_specs=[cut(rows // 2)] * 4,
         compiler_params=kernel_room,
         cost_estimate=pl.CostEstimate(
-            flops=0, bytes_accessed=2 * rows * width * (len(terms) + 2), transcendentals=0
+            flops=0, bytes_accessed=4 * rows * width * (n + 2), transcendentals=0
         ),
-    )(*terms)
+    )(*first, *second)
 
 
 def core_add_kernel(n, *refs):
@@ -676,8 +680,7 @@
     )
     inner_q, inner_p, p_terms, packet = barrier((inner_q, inner_p, p_terms, packet))
     everything = lax.all_to_all(packet, everyone, 0, 0).reshape(n_all * n_seq8, -1)
-    q_own, q_away = ring_add(q_terms)
-    p_own, p_away = ring_add(p_terms)
+    q_own, q_away, p_own, p_away = ring_add(q_terms, p_terms)
     keep, give = down_parts(spot, tok_q, tok_p, inner_q, inner_p, d_own)
     keep, give, q_own, q_away, p_own, p_away, everything = barrier(
         (keep, give, q_own, q_away, p_own, p_away, everything)

time: 253 us -> 252 us (level)
  transfers between devices with their start and end apart: 57 -> 57, of which waited for: 22 -> 24; matrix products, arithmetic and copies ran while one was open for 9% -> 9% of each run, Pallas kernels for 24% -> 24%
where the time goes in v2:
time: 252 us; the launch traced here: 251 us
  starting transfers between devices  86.6 us (34%)
  waiting for transfers between devices  68.7 us (27%)
  Pallas kernels  60.2 us (24%)
  local copies, waits for them, and re-layouts  19.2 us (8%)
  other arithmetic  14.5 us (6%)
    ppermute x25, starting transfers between devices, shift(): lax.ppermute(value, axis, [(i, (i + step) % size) for i in range(size)])  39.6 us
    ppermute x25, waiting for transfers between devices, shift(): lax.ppermute(value, axis, [(i, (i + step) % size) for i in range(size)])  29.2 us
    ppermute x26, waiting for transfers between devices, swap(): return lax.ppermute(value, axis, swap2)  17.2 us
    all_to_all x2, starting transfers between devices, spread(): lax.all_to_all(jnp.broadcast_to(block[None], (count,) + block.shape), axe...  13 us
    ppermute x26, starting transfers between devices, swap(): return lax.ppermute(value, axis, swap2)  11.9 us
    pallas_call x1, Pallas kernels, token_half(): pl.pallas_call(lambda *refs: token_kernel(n_seq, len(blocks), *refs), gri...  11.3 us
    all_to_all x1, waiting for transfers between devices, per_device(): arrived = lax.all_to_all(chip_sum, chips, 0, 0)  9.49 us
    pallas_call x1, Pallas kernels, down_parts(): pl.pallas_call(down_kernel, grid=(steps,), out_shape=[jax.ShapeDtypeStruc...  9.31 us
  transfers between devices with their start and end apart: 57, of which 24 were waited for; matrix products, arithmetic and copies ran while one was open for 9% of the time, Pallas kernels for 24%

profile of v2, /device:TPU:0, one launch (start us, length us, event | category | flops | bytes accessed | tf_op | source)
XLA Modules:
  0.0 250.7 jit_solution(8481472346931763860)
XLA Ops:
  0.7 3.4 %collective-permute-start = (bf16[32,4096]{1,0:T(8,128)(2,1)}, bf16[32,4096]{1,0:T(8,128)(2,1)S(1)}, u32[]{:S(2)}, u32[]{:S(2)}) collective-permute-start(bf16[32,4096]{1,0:T(8,128)(2,1)} %bitcast.68), channel_id=1, source_target_pairs={{0,2},{2,0},{1,3},{3,1},{4,6},{6,4},{5,7},{7,5},{8,10},{10,8},{9,1... | collective-permute-start | bytes 786440 | tf_op jit(solution)/shard_map/ppermute | solution.py:22
  6.2 5.5 %collective-permute-done = bf16[32,4096]{1,0:T(8,128)(2,1)S(1)} collective-permute-done((bf16[32,4096]{1,0:T(8,128)(2,1)}, bf16[32,4096]{1,0:T(8,128)(2,1)S(1)}, u32[]{:S(2)}, u32[]{:S(2)}) %collective-permute-start) | collective-permute-done | bytes 262176 | tf_op jit(solution)/shard_map/ppermute | solution.py:22
  11.6 4.9 %collective-permute-done.1 = bf16[32,4096]{1,0:T(8,128)(2,1)S(1)} collective-permute-done((bf16[32,4096]{1,0:T(8,128)(2,1)}, bf16[32,4096]{1,0:T(8,128)(2,1)S(1)}, u32[]{:S(2)}, u32[]{:S(2)}) %collective-permute-start.1) | collective-permute-done | bytes 262176 | tf_op jit(solution)/shard_map/ppermute | solution.py:22
  26.3 5.3 %collective-permute-done.6.refs_6_.refs_10_.refs_2_ = bf16[64,4096]{1,0:T(8,128)(2,1)S(1)} collective-permute-done((bf16[64,4096]{1,0:T(8,128)(2,1)S(1)}, bf16[64,4096]{1,0:T(8,128)(2,1)S(1)}, u32[]{:S(2)}, u32[]{:S(2)}) %collective-permute-start.6) | collective-permute-done | bytes 524320 | tf_op jit(solution)/shard_map/ppermute | solution.py:18
  33.4 3.0 %collective-permute-start.9 = (bf16[32,4096]{1,0:T(8,128)(2,1)}, bf16[32,4096]{1,0:T(8,128)(2,1)}, u32[]{:S(2)}, u32[]{:S(2)}) collective-permute-start(bf16[32,4096]{1,0:T(8,128)(2,1)} %slice.91), channel_id=1, source_target_pairs={{0,96},{32,0},{64,32},{96,64},{1,97},{33,1},{65,33},{97,65},{2,98}... | collective-permute-start | bytes 786440 | tf_op jit(solution)/shard_map/ppermute | solution.py:18
  48.6 6.3 %all-to-all-start = ((bf16[16,64,512]{2,1,0:T(8,128)(2,1)}), bf16[16,64,512]{2,1,0:T(8,128)(2,1)}, u32[]{:S(2)}, u32[]{:S(2)}) async-start(bf16[16,64,512]{2,1,0:T(8,128)(2,1)} %broadcast_in_dim.139), calls=%async_computation | async-start | bytes 2097152 | tf_op jit(solution)/shard_map/all_to_all | solution.py:533
  60.2 5.1 %shard_map.137 = (f32[256,512]{1,0:T(8,128)}, f32[256,1]{1,0:T(8,128)}, f32[256,1]{1,0:T(8,128)}) custom-call(bf16[64,4096]{1,0:T(8,128)(2,1)} %copy-done.6, bf16[64,4096]{1,0:T(8,128)(2,1)} %copy-done.7, bf16[32,4096]{1,0:T(8,128)(2,1)} %collective-permute-done.3.refs_2_.refs_6_.refs_3_, bf16[32,4096]{1,0:T(8,128)(2,1)} %collective-permute-done.5.refs_3_.refs_7_.refs_4_, ...), custom_call_target="tpu_custom_call" | custom-call | tf_op jit(solution)/shard_map/pallas_call | solution.py:112
  69.5 3.2 %collective-permute-start.16 = (bf16[2,4,2,32,512]{4,3,2,1,0:T(8,128)(2,1)S(1)}, bf16[2,4,2,32,512]{4,3,2,1,0:T(8,128)(2,1)S(1)}, u32[]{:S(2)}, u32[]{:S(2)}) collective-permute-start(bf16[2,4,2,32,512]{4,3,2,1,0:T(8,128)(2,1)S(1)} %get-tuple-element.230.refs_1_), channel_id=1, source_target_pairs={{0,96},{32,0},{64,32},{96,64},{1,97},{33,1},{65,33},{97,65},{2,98}... | collective-permute-start | bytes 1572872 | tf_op jit(solution)/shard_map/ppermute | solution.py:18
  73.5 6.7 %all-to-all-start.1 = ((f32[8,1,640]{2,1,0:T(1,128)}), f32[8,1,640]{2,1,0:T(1,128)S(1)}, u32[]{:S(2)}, u32[]{:S(2)}) async-start(f32[8,1,640]{2,1,0:T(1,128)} %broadcast_in_dim.140), calls=%async_computation.1 | async-start | bytes 40960 | tf_op jit(solution)/shard_map/all_to_all | solution.py:533
  80.9 3.2 %collective-permute-start.18 = (bf16[2,4,2,32,512]{4,3,2,1,0:T(8,128)(2,1)S(1)}, bf16[2,4,2,32,512]{4,3,2,1,0:T(8,128)(2,1)S(1)}, u32[]{:S(2)}, u32[]{:S(2)}) collective-permute-start(bf16[2,4,2,32,512]{4,3,2,1,0:T(8,128)(2,1)S(1)} %get-tuple-element.224.refs_1_), channel_id=1, source_target_pairs={{0,96},{32,0},{64,32},{96,64},{1,97},{33,1},{65,33},{97,65},{2,98}... | collective-permute-start | bytes 1572872 | tf_op jit(solution)/shard_map/ppermute | solution.py:18
  84.1 3.7 %all-to-all-done.1 = f32[8,1,640]{2,1,0:T(1,128)S(1)} async-done(((f32[8,1,640]{2,1,0:T(1,128)}), f32[8,1,640]{2,1,0:T(1,128)S(1)}, u32[]{:S(2)}, u32[]{:S(2)}) %all-to-all-start.1) | async-done | bytes 20512 | tf_op jit(solution)/shard_map/all_to_all | solution.py:533
  89.3 6.3 %shard_map.138 = (bf16[256,512]{1,0:T(8,128)(2,1)}, bf16[8,4,4096]{2,1,0:T(4,128)(2,1)}, bf16[16,2,4096]{2,1,0:T(2,128)(2,1)}) custom-call(s32[17]{0:T(128)} %concatenate.40.refs_0_.core, f32[256,512]{1,0:T(8,128)} %get-tuple-element.174.refs_1_, f32[256,3]{1,0:T(8,128)} %copy.42.refs_2_, s32[1,512]{1,0:T(1,128)} %add.343.refs_3_, ...), custom_call_target="tpu_custom_call" | custom-call | tf_op jit(solution)/shard_map/pallas_call | solution.py:167
  95.6 3.8 %all-to-all-start.2 = ((bf16[8,4,4096]{2,1,0:T(4,128)(2,1)}), bf16[8,4,4096]{2,1,0:T(4,128)(2,1)S(1)}, u32[]{:S(2)}, u32[]{:S(2)}) async-start(bf16[8,4,4096]{2,1,0:T(4,128)(2,1)} %get-tuple-element.183), calls=%async_computation.2 | async-start | bytes 524288 | tf_op jit(solution)/shard_map/all_to_all | solution.py:638
  100.2 4.4 %shard_map.139 = (bf16[64,4096]{1,0:T(8,128)(2,1)}, bf16[64,4096]{1,0:T(8,128)(2,1)}, bf16[64,4096]{1,0:T(8,128)(2,1)}, bf16[64,4096]{1,0:T(8,128)(2,1)}) custom-call(bf16[256,512]{1,0:T(8,128)(2,1)} %get-tuple-element.190.refs_0_, bf16[64,4096]{1,0:T(8,128)(2,1)} %copy-done, bf16[64,4096]{1,0:T(8,128)(2,1)} %copy-done.1, bf16[32,4096]{1,0:T(8,128)(2,1)} %copy-done.8, ...), custom_call_target="tpu_custom_call" | custom-call | flops 1073741824 | bytes 6291456 | tf_op jit(solution)/shard_map/pallas_call | solution.py:287
  104.7 3.5 %all-to-all-done.2 = bf16[8,4,4096]{2,1,0:T(4,128)(2,1)S(1)} async-done(((bf16[8,4,4096]{2,1,0:T(4,128)(2,1)}), bf16[8,4,4096]{2,1,0:T(4,128)(2,1)S(1)}, u32[]{:S(2)}, u32[]{:S(2)}) %all-to-all-start.2) | async-done | bytes 262176 | tf_op jit(solution)/shard_map/all_to_all | solution.py:638
  111.5 3.0 %collective-permute-start.20 = (bf16[1,4,2,32,512]{4,3,2,1,0:T(8,128)(2,1)}, bf16[1,4,2,32,512]{4,3,2,1,0:T(8,128)(2,1)S(1)}, u32[]{:S(2)}, u32[]{:S(2)}) collective-permute-start(bf16[1,4,2,32,512]{4,3,2,1,0:T(8,128)(2,1)} %slice.77), channel_id=1, source_target_pairs={{0,96},{32,0},{64,32},{96,64},{1,97},{33,1},{65,33},{97,65},{2,98}... | collective-permute-start | bytes 786440 | tf_op jit(solution)/shard_map/ppermute | solution.py:18
  114.4 3.5 %all-to-all-start.3 = ((bf16[16,2,4096]{2,1,0:T(2,128)(2,1)}), bf16[16,2,4096]{2,1,0:T(2,128)(2,1)S(1)}, u32[]{:S(2)}, u32[]{:S(2)}) async-start(bf16[16,2,4096]{2,1,0:T(2,128)(2,1)} %get-tuple-element.189), calls=%async_computation.3 | async-start | bytes 524288 | tf_op jit(solution)/shard_map/all_to_all | solution.py:637
  117.9 4.2 %shard_map.140 = (bf16[64,4096]{1,0:T(8,128)(2,1)}, bf16[64,4096]{1,0:T(8,128)(2,1)}, bf16[64,4096]{1,0:T(8,128)(2,1)}, bf16[64,4096]{1,0:T(8,128)(2,1)}, bf16[6...) custom-call(bf16[256,512]{1,0:T(8,128)(2,1)} %get-tuple-element.190.refs_0_,, ...), custom_call_target="tpu_custom_call" | custom-call | flops 1073741824 | bytes 6291456 | tf_op jit(solution)/shard_map/pallas_call | solution.py:287
  125.7 7.5 %collective-permute-done.23.refs_3_ = bf16[64,4096]{1,0:T(8,128)(2,1)} collective-permute-done((bf16[64,4096]{1,0:T(8,128)(2,1)}, bf16[64,4096]{1,0:T(8,128)(2,1)}, u32[]{:S(2)}, u32[]{:S(2)}) %collective-permute-start.23) | collective-permute-done | bytes 524320 | tf_op jit(solution)/shard_map/ppermute | solution.py:18
  140.1 3.3 %shard_map.141 = (bf16[64,4096]{1,0:T(8,128)(2,1)}, bf16[64,4096]{1,0:T(8,128)(2,1)}, bf16[64,4096]{1,0:T(8,128)(2,1)}, bf16[64,4096]{1,0:T(8,128)(2,1)}) custom-call(bf16[64,4096]{1,0:T(8,128)(2,1)} %get-tuple-element.210.refs_0_, bf16[64,4096]{1,0:T(8,128)(2,1)} %get-tuple-element.211.refs_1_, bf16[64,4096]{1,0:T(8,128)(2,1)} %get-tuple-element.212.refs_2_, ...), custom_call_target="tpu_custom_call" | custom-call | tf_op jit(solution)/shard_map/pallas_call | solution.py:227
  149.8 11.3 %shard_map.143 = (f32[128,512]{1,0:T(8,128)}, f32[768,512]{1,0:T(8,128)}, f32[8,512]{1,0:T(8,128)}) custom-call(s32[17]{0:T(128)} %concatenate.40.refs_0_.core, bf16[2,4,2,32,512]{4,3,2,1,0:T(8,128)(2,1)} %copy-done.12, bf16[2,4,2,32,512]{4,3,2,1,0:T(8,128)(2,1)} %copy-done.13, bf16[1,4,2,32,512]{4,3,2,1,0:T(8,128)(2,1)} %collective-permute-done.19.refs_3_, ...), custom_call_target="tpu_custom_call" | custom-call | tf_op jit(solution)/shard_map/pallas_call | solution.py:429
  161.9 4.5 %shard_map.142 = f32[16,256]{1,0:T(8,128)} custom-call(bf16[16,4096]{1,0:T(8,128)(2,1)} %pad_maximum_fusion.3.refs_0_, bf16[2,4,2,32,512]{4,3,2,1,0:T(8,128)(2,1)} %copy-done.11, bf16[2,4,2,32,512]{4,3,2,1,0:T(8,128)(2,1)} %copy-done.15, bf16[1,4,2,32,512]{4,3,2,1,0:T(8,128)(2,1)} %copy-done.29, bf16[1,4,2,32,512]{4,3,2,1,0:T(8,128)(2,1)} %copy-done.30, ...), custom_call_target="tpu_custom_call" | custom-call | tf_op jit(solution)/shard_map/pallas_call | solution.py:490
  169.5 4.2 %shard_map.144 = (bf16[128,512]{1,0:T(8,128)(2,1)}, bf16[768,512]{1,0:T(8,128)(2,1)}) custom-call(s32[17]{0:T(128)} %concatenate.40.refs_0_.core, f32[8,256]{1,0:T(8,128)} %get-tuple-element.304.refs_1_, f32[8,256]{1,0:T(8,128)} %copy-done.35, bf16[512,512]{1,0:T(8,128)(2,1)} %fusion.refs_3_, f32[128,512]{1,0:T(8,128)} %get-tuple-element.240.refs_4_, ...), custom_call_target="tpu_custom_call" | custom-call | tf_op jit(solution)/shard_map/pallas_call | solution.py:522
  173.8 7.9 %all-to-all-start.4 = ((bf16[128,8,384]{2,1,0:T(8,128)(2,1)}), bf16[128,8,384]{2,1,0:T(8,128)(2,1)S(1)}, u32[]{:S(2)}, u32[]{:S(2)}) async-start(bf16[128,8,384]{2,1,0:T(8,128)(2,1)} %bitcast.18), calls=%async_computation.4 | async-start | bytes 1572864 | tf_op jit(solution)/shard_map/all_to_all | solution.py:682
  181.7 4.2 %shard_map.146 = (f32[32,4096]{1,0:T(8,128)}, bf16[32,4096]{1,0:T(8,128)(2,1)}, f32[32,4096]{1,0:T(8,128)}, bf16[32,4096]{1,0:T(8,128)(2,1)}) custom-call(bf16[64,4096]{1,0:T(8,128)(2,1)} %get-tuple-element.256.refs_0_, bf16[64,4096]{1,0:T(8,128)(2,1)} %collective-permute-done.21.refs_1_, bf16[64,4096]{1,0:T(8,128)(2,1)} %collective-permute-done.22.refs_2_, ...), custom_call_target="tpu_custom_call" | custom-call | bytes 6291456 | tf_op jit(solution)/shard_map/pallas_call | solution.py:202
  185.9 9.3 %shard_map.145 = (bf16[64,32,512]{2,1,0:T(8,128)(2,1)}, bf16[16,32,512]{2,1,0:T(8,128)(2,1)}, bf16[16,32,512]{2,1,0:T(8,128)(2,1)}, bf16[16,32,512]{2,1,0:T(8,128)(2,1)}, bf16[16,32,512]{2,1,0:T(8,128)(2,1)}) custom-call(s32[17]{0:T(128)} %concatenate.40.refs_0_.core, bf16[128,4096]{1,0:T(8,128)(2,1)} %bitcast.64, bf16[768,4096]{1,0:T(8,128)(2,1)} %bitcast.61, ...), custom_call_target="tpu_custom_call" | custom-call | flops 3758096384 | bytes 8388608 | tf_op jit(solution)/shard_map/pallas_call | solution.py:341
  195.2 2.9 %all-to-all-done.4 = bf16[128,8,384]{2,1,0:T(8,128)(2,1)S(1)} async-done(((bf16[128,8,384]{2,1,0:T(8,128)(2,1)}), bf16[128,8,384]{2,1,0:T(8,128)(2,1)S(1)}, u32[]{:S(2)}, u32[]{:S(2)}) %all-to-all-start.4) | async-done | bytes 786464 | tf_op jit(solution)/shard_map/all_to_all | solution.py:682
  200.9 4.4 %collective-permute-done.47 = f32[4,4,2,256]{3,2,1,0:T(2,128)S(1)} collective-permute-done((f32[4,4,2,256]{3,2,1,0:T(2,128)S(1)}, f32[4,4,2,256]{3,2,1,0:T(2,128)S(1)}, u32[]{:S(2)}, u32[]{:S(2)}) %collective-permute-start.47) | collective-permute-done | bytes 32800 | tf_op jit(solution)/shard_map/ppermute | solution.py:22
  209.9 3.4 %shard_map.147 = bf16[64,32,512]{2,1,0:T(8,128)(2,1)} custom-call(bf16[64,32,512]{2,1,0:T(8,128)(2,1)} %get-tuple-element.273.refs_0_, bf16[16,32,512]{2,1,0:T(8,128)(2,1)} %copy-done.17, bf16[16,32,512]{2,1,0:T(8,128)(2,1)} %copy-done.18, bf16[16,32,512]{2,1,0:T(8,128)(2,1)} %copy-done.19, bf16[16,32,512]{2,1,0:T(8,128)(2,1)} %copy-done.20), custom_call_target="tpu_custom_call" | custom-call | tf_op jit(solution)/shard_map/pallas_call | solution.py:253
  213.3 6.9 %all-to-all-start.5 = ((bf16[64,32,512]{2,1,0:T(8,128)(2,1)}), bf16[64,32,512]{2,1,0:T(8,128)(2,1)S(1)}, u32[]{:S(2)}, u32[]{:S(2)}) async-start(bf16[64,32,512]{2,1,0:T(8,128)(2,1)} %shard_map.147), calls=%async_computation.5 | async-start | bytes 4194304 | tf_op jit(solution)/shard_map/all_to_all | solution.py:707
  229.8 9.1 %collective-permute-done.49 = f32[4,4,256]{2,1,0:T(4,128)S(1)} collective-permute-done((f32[4,4,256]{2,1,0:T(4,128)S(1)}, f32[4,4,256]{2,1,0:T(4,128)S(1)}, u32[]{:S(2)}, u32[]{:S(2)}) %collective-permute-start.49) | collective-permute-done | bytes 16416 | tf_op jit(solution)/shard_map/ppermute | solution.py:18
  239.6 9.5 %all-to-all-done.5 = bf16[64,32,512]{2,1,0:T(8,128)(2,1)S(1)} async-done(((bf16[64,32,512]{2,1,0:T(8,128)(2,1)}), bf16[64,32,512]{2,1,0:T(8,128)(2,1)S(1)}, u32[]{:S(2)}, u32[]{:S(2)}) %all-to-all-start.5) | async-done | bytes 2097184 | tf_op jit(solution)/shard_map/all_to_all | solution.py:707
  (256 shorter events, 82.1 us)
Async XLA Ops:
  4.0 12.5 %collective-permute-start.1 = (bf16[32,4096]{1,0:T(8,128)(2,1)}, bf16[32,4096]{1,0:T(8,128)(2,1)S(1)}, u32[]{:S(2)}, u32[]{:S(2)}) collective-permute-start(bf16[32,4096]{1,0:T(8,128)(2,1)} %bitcast.66), channel_id=1, source_target_pairs={{0,16},{16,0},{1,17},{17,1},{2,18},{18,2},{3,19},{19,3},{4,20},{20... | collective-permute-start | bytes 786440 | tf_op jit(solution)/shard_map/ppermute | solution.py:22
  17.5 14.1 %collective-permute-start.6 = (bf16[64,4096]{1,0:T(8,128)(2,1)S(1)}, bf16[64,4096]{1,0:T(8,128)(2,1)S(1)}, u32[]{:S(2)}, u32[]{:S(2)}) collective-permute-start(bf16[64,4096]{1,0:T(8,128)(2,1)S(1)} %pad_maximum_fusion.2.refs_5_.refs_9_.refs_1_), channel_id=1, source_target_pairs={{0,32},{32,64},{64,96},{96,0},{1,33},{33,65},{65,97},{97,1},{2,34}... | collective-permute-start | bytes 1572872 | tf_op jit(solution)/shard_map/ppermute | solution.py:18
  19.1 13.6 %collective-permute-start.8 = (bf16[64,4096]{1,0:T(8,128)(2,1)S(1)}, bf16[64,4096]{1,0:T(8,128)(2,1)S(1)}, u32[]{:S(2)}, u32[]{:S(2)}) collective-permute-start(bf16[64,4096]{1,0:T(8,128)(2,1)S(1)} %pad_maximum_fusion.2.refs_5_.refs_9_.refs_1_), channel_id=1, source_target_pairs={{0,96},{32,0},{64,32},{96,64},{1,97},{33,1},{65,33},{97,65},{2,98}... | collective-permute-start | bytes 1572872 | tf_op jit(solution)/shard_map/ppermute | solution.py:18
  21.8 14.6 %collective-permute-start.2 = (bf16[64,4096]{1,0:T(8,128)(2,1)S(1)}, bf16[64,4096]{1,0:T(8,128)(2,1)S(1)}, u32[]{:S(2)}, u32[]{:S(2)}) collective-permute-start(bf16[64,4096]{1,0:T(8,128)(2,1)S(1)} %pad_maximum_fusion.1.refs_0_.refs_4_.refs_1_), channel_id=1, source_target_pairs={{0,4},{4,8},{8,12},{12,0},{1,5},{5,9},{9,13},{13,1},{2,6},{6,10},{... | collective-permute-start | bytes 1572872 | tf_op jit(solution)/shard_map/ppermute | solution.py:18
  23.8 15.3 %collective-permute-start.4 = (bf16[64,4096]{1,0:T(8,128)(2,1)S(1)}, bf16[64,4096]{1,0:T(8,128)(2,1)}, u32[]{:S(2)}, u32[]{:S(2)}) collective-permute-start(bf16[64,4096]{1,0:T(8,128)(2,1)S(1)} %pad_maximum_fusion.1.refs_0_.refs_4_.refs_1_), channel_id=1, source_target_pairs={{0,12},{4,0},{8,4},{12,8},{1,13},{5,1},{9,5},{13,9},{2,14},{6,2},{... | collective-permute-start | bytes 1572872 | tf_op jit(solution)/shard_map/ppermute | solution.py:18
  26.0 18.5 %collective-permute-start.10 = (bf16[64,4096]{1,0:T(8,128)(2,1)S(1)}, bf16[64,4096]{1,0:T(8,128)(2,1)S(1)}, u32[]{:S(2)}, u32[]{:S(2)}) collective-permute-start(bf16[64,4096]{1,0:T(8,128)(2,1)S(1)} %pad_maximum_fusion.2.refs_5_.refs_9_.refs_1_), channel_id=1, source_target_pairs={{0,1},{1,0},{2,3},{3,2},{4,5},{5,4},{6,7},{7,6},{8,9},{9,8},{10,11... | collective-permute-start | bytes 1572872 | tf_op jit(solution)/shard_map/ppermute | solution.py:22
  32.4 12.1 %collective-permute-start.7 = (bf16[32,4096]{1,0:T(8,128)(2,1)}, bf16[32,4096]{1,0:T(8,128)(2,1)S(1)}, u32[]{:S(2)}, u32[]{:S(2)}) collective-permute-start(bf16[32,4096]{1,0:T(8,128)(2,1)} %slice.90), channel_id=1, source_target_pairs={{0,32},{32,64},{64,96},{96,0},{1,33},{33,65},{65,97},{97,1},{2,34}... | collective-permute-start | bytes 786440 | tf_op jit(solution)/shard_map/ppermute | solution.py:18
  33.4 11.1 %collective-permute-start.9 = (bf16[32,4096]{1,0:T(8,128)(2,1)}, bf16[32,4096]{1,0:T(8,128)(2,1)}, u32[]{:S(2)}, u32[]{:S(2)}) collective-permute-start(bf16[32,4096]{1,0:T(8,128)(2,1)} %slice.91), channel_id=1, source_target_pairs={{0,96},{32,0},{64,32},{96,64},{1,97},{33,1},{65,33},{97,65},{2,98}... | collective-permute-start | bytes 786440 | tf_op jit(solution)/shard_map/ppermute | solution.py:18
  48.6 19.5 %all-to-all-start = ((bf16[16,64,512]{2,1,0:T(8,128)(2,1)}), bf16[16,64,512]{2,1,0:T(8,128)(2,1)}, u32[]{:S(2)}, u32[]{:S(2)}) async-start(bf16[16,64,512]{2,1,0:T(8,128)(2,1)} %broadcast_in_dim.139), calls=%async_computation | async-start | bytes 2097152 | tf_op jit(solution)/shard_map/all_to_all | solution.py:533
  69.4 18.5 %collective-permute-start.15 = (bf16[2,4,2,32,512]{4,3,2,1,0:T(8,128)(2,1)S(1)}, bf16[2,4,2,32,512]{4,3,2,1,0:T(8,128)(2,1)S(1)}, u32[]{:S(2)}, u32[]{:S(2)}) collective-permute-start(bf16[2,4,2,32,512]{4,3,2,1,0:T(8,128)(2,1)S(1)} %get-tuple-element.230.refs_1_), channel_id=1, source_target_pairs={{0,32},{32,64},{64,96},{96,0},{1,33},{33,65},{65,97},{97,1},{2,34}... | collective-permute-start | bytes 1572872 | tf_op jit(solution)/shard_map/ppermute | solution.py:18
  69.5 18.4 %collective-permute-start.16 = (bf16[2,4,2,32,512]{4,3,2,1,0:T(8,128)(2,1)S(1)}, bf16[2,4,2,32,512]{4,3,2,1,0:T(8,128)(2,1)S(1)}, u32[]{:S(2)}, u32[]{:S(2)}) collective-permute-start(bf16[2,4,2,32,512]{4,3,2,1,0:T(8,128)(2,1)S(1)} %get-tuple-element.230.refs_1_), channel_id=1, source_target_pairs={{0,96},{32,0},{64,32},{96,64},{1,97},{33,1},{65,33},{97,65},{2,98}... | collective-permute-start | bytes 1572872 | tf_op jit(solution)/shard_map/ppermute | solution.py:18
  73.5 14.4 %all-to-all-start.1 = ((f32[8,1,640]{2,1,0:T(1,128)}), f32[8,1,640]{2,1,0:T(1,128)S(1)}, u32[]{:S(2)}, u32[]{:S(2)}) async-start(f32[8,1,640]{2,1,0:T(1,128)} %broadcast_in_dim.140), calls=%async_computation.1 | async-start | bytes 40960 | tf_op jit(solution)/shard_map/all_to_all | solution.py:533
  80.9 23.7 %collective-permute-start.17 = (bf16[2,4,2,32,512]{4,3,2,1,0:T(8,128)(2,1)S(1)}, bf16[2,4,2,32,512]{4,3,2,1,0:T(8,128)(2,1)S(1)}, u32[]{:S(2)}, u32[]{:S(2)}) collective-permute-start(bf16[2,4,2,32,512]{4,3,2,1,0:T(8,128)(2,1)S(1)} %get-tuple-element.224.refs_1_), channel_id=1, source_target_pairs={{0,32},{32,64},{64,96},{96,0},{1,33},{33,65},{65,97},{97,1},{2,34}... | collective-permute-start | bytes 1572872 | tf_op jit(solution)/shard_map/ppermute | solution.py:18
  80.9 23.8 %collective-permute-start.18 = (bf16[2,4,2,32,512]{4,3,2,1,0:T(8,128)(2,1)S(1)}, bf16[2,4,2,32,512]{4,3,2,1,0:T(8,128)(2,1)S(1)}, u32[]{:S(2)}, u32[]{:S(2)}) collective-permute-start(bf16[2,4,2,32,512]{4,3,2,1,0:T(8,128)(2,1)S(1)} %get-tuple-element.224.refs_1_), channel_id=1, source_target_pairs={{0,96},{32,0},{64,32},{96,64},{1,97},{33,1},{65,33},{97,65},{2,98}... | collective-permute-start | bytes 1572872 | tf_op jit(solution)/shard_map/ppermute | solution.py:18
  95.6 12.5 %all-to-all-start.2 = ((bf16[8,4,4096]{2,1,0:T(4,128)(2,1)}), bf16[8,4,4096]{2,1,0:T(4,128)(2,1)S(1)}, u32[]{:S(2)}, u32[]{:S(2)}) async-start(bf16[8,4,4096]{2,1,0:T(4,128)(2,1)} %get-tuple-element.183), calls=%async_computation.2 | async-start | bytes 524288 | tf_op jit(solution)/shard_map/all_to_all | solution.py:638
  100.1 11.3 %collective-permute-start.19 = (bf16[1,4,2,32,512]{4,3,2,1,0:T(8,128)(2,1)}, bf16[1,4,2,32,512]{4,3,2,1,0:T(8,128)(2,1)}, u32[]{:S(2)}, u32[]{:S(2)}) collective-permute-start(bf16[1,4,2,32,512]{4,3,2,1,0:T(8,128)(2,1)} %slice.76), channel_id=1, source_target_pairs={{0,32},{32,64},{64,96},{96,0},{1,33},{33,65},{65,97},{97,1},{2,34}... | collective-permute-start | bytes 786440 | tf_op jit(solution)/shard_map/ppermute | solution.py:18
  108.2 15.2 %collective-permute-start.21 = (bf16[64,4096]{1,0:T(8,128)(2,1)}, bf16[64,4096]{1,0:T(8,128)(2,1)}, u32[]{:S(2)}, u32[]{:S(2)}) collective-permute-start(bf16[64,4096]{1,0:T(8,128)(2,1)} %get-tuple-element.204), channel_id=1, source_target_pairs={{0,12},{4,0},{8,4},{12,8},{1,13},{5,1},{9,5},{13,9},{2,14},{6,2},{... | collective-permute-start | bytes 1572872 | tf_op jit(solution)/shard_map/ppermute | solution.py:18
  109.0 16.7 %collective-permute-start.22 = (bf16[64,4096]{1,0:T(8,128)(2,1)}, bf16[64,4096]{1,0:T(8,128)(2,1)}, u32[]{:S(2)}, u32[]{:S(2)}) collective-permute-start(bf16[64,4096]{1,0:T(8,128)(2,1)} %get-tuple-element.205), channel_id=1, source_target_pairs={{0,8},{4,12},{8,0},{12,4},{1,9},{5,13},{9,1},{13,5},{2,10},{6,14},... | collective-permute-start | bytes 1572872 | tf_op jit(solution)/shard_map/ppermute | solution.py:18
  110.5 22.7 %collective-permute-start.23 = (bf16[64,4096]{1,0:T(8,128)(2,1)}, bf16[64,4096]{1,0:T(8,128)(2,1)}, u32[]{:S(2)}, u32[]{:S(2)}) collective-permute-start(bf16[64,4096]{1,0:T(8,128)(2,1)} %get-tuple-element.206), channel_id=1, source_target_pairs={{0,4},{4,8},{8,12},{12,0},{1,5},{5,9},{9,13},{13,1},{2,6},{6,10},{... | collective-permute-start | bytes 1572872 | tf_op jit(solution)/shard_map/ppermute | solution.py:18
  110.7 23.0 %collective-permute-start.25 = (bf16[2,4,2,32,512]{4,3,2,1,0:T(8,128)(2,1)S(1)}, bf16[2,4,2,32,512]{4,3,2,1,0:T(8,128)(2,1)}, u32[]{:S(2)}, u32[]{:S(2)}) collective-permute-start(bf16[2,4,2,32,512]{4,3,2,1,0:T(8,128)(2,1)S(1)} %get-tuple-element.230.refs_1_), channel_id=1, source_target_pairs={{0,1},{1,0},{2,3},{3,2},{4,5},{5,4},{6,7},{7,6},{8,9},{9,8},{10,11... | collective-permute-start | bytes 1572872 | tf_op jit(solution)/shard_map/ppermute | solution.py:22
  114.4 11.2 %all-to-all-start.3 = ((bf16[16,2,4096]{2,1,0:T(2,128)(2,1)}), bf16[16,2,4096]{2,1,0:T(2,128)(2,1)S(1)}, u32[]{:S(2)}, u32[]{:S(2)}) async-start(bf16[16,2,4096]{2,1,0:T(2,128)(2,1)} %get-tuple-element.189), calls=%async_computation.3 | async-start | bytes 524288 | tf_op jit(solution)/shard_map/all_to_all | solution.py:637
  122.4 12.5 %collective-permute-start.26 = (bf16[2,4,2,32,512]{4,3,2,1,0:T(8,128)(2,1)S(1)}, bf16[2,4,2,32,512]{4,3,2,1,0:T(8,128)(2,1)}, u32[]{:S(2)}, u32[]{:S(2)}) collective-permute-start(bf16[2,4,2,32,512]{4,3,2,1,0:T(8,128)(2,1)S(1)} %collective-permute-done.15.refs_2_), channel_id=1, source_target_pairs={{0,1},{1,0},{2,3},{3,2},{4,5},{5,4},{6,7},{7,6},{8,9},{9,8},{10,11... | collective-permute-start | bytes 1572872 | tf_op jit(solution)/shard_map/ppermute | solution.py:22
  123.4 12.1 %collective-permute-start.29 = (bf16[2,4,2,32,512]{4,3,2,1,0:T(8,128)(2,1)S(1)}, bf16[2,4,2,32,512]{4,3,2,1,0:T(8,128)(2,1)}, u32[]{:S(2)}, u32[]{:S(2)}) collective-permute-start(bf16[2,4,2,32,512]{4,3,2,1,0:T(8,128)(2,1)S(1)} %collective-permute-done.16.refs_5_), channel_id=1, source_target_pairs={{0,1},{1,0},{2,3},{3,2},{4,5},{5,4},{6,7},{7,6},{8,9},{9,8},{10,11... | collective-permute-start | bytes 1572872 | tf_op jit(solution)/shard_map/ppermute | solution.py:22
  145.2 28.5 %collective-permute-start.37 = (bf16[64,4096]{1,0:T(8,128)(2,1)}, bf16[64,4096]{1,0:T(8,128)(2,1)S(1)}, u32[]{:S(2)}, u32[]{:S(2)}) collective-permute-start(bf16[64,4096]{1,0:T(8,128)(2,1)} %get-tuple-element.245), channel_id=1, source_target_pairs={{0,96},{32,0},{64,32},{96,64},{1,97},{33,1},{65,33},{97,65},{2,98}... | collective-permute-start | bytes 1572872 | tf_op jit(solution)/shard_map/ppermute | solution.py:18
  148.0 25.8 %collective-permute-start.38 = (bf16[64,4096]{1,0:T(8,128)(2,1)}, bf16[64,4096]{1,0:T(8,128)(2,1)S(1)}, u32[]{:S(2)}, u32[]{:S(2)}) collective-permute-start(bf16[64,4096]{1,0:T(8,128)(2,1)} %get-tuple-element.246), channel_id=1, source_target_pairs={{0,64},{32,96},{64,0},{96,32},{1,65},{33,97},{65,1},{97,33},{2,66}... | collective-permute-start | bytes 1572872 | tf_op jit(solution)/shard_map/ppermute | solution.py:18
  149.1 24.7 %collective-permute-start.39 = (bf16[64,4096]{1,0:T(8,128)(2,1)}, bf16[64,4096]{1,0:T(8,128)(2,1)S(1)}, u32[]{:S(2)}, u32[]{:S(2)}) collective-permute-start(bf16[64,4096]{1,0:T(8,128)(2,1)} %get-tuple-element.247), channel_id=1, source_target_pairs={{0,32},{32,64},{64,96},{96,0},{1,33},{33,65},{65,97},{97,1},{2,34}... | collective-permute-start | bytes 1572872 | tf_op jit(solution)/shard_map/ppermute | solution.py:18
  173.8 24.3 %all-to-all-start.4 = ((bf16[128,8,384]{2,1,0:T(8,128)(2,1)}), bf16[128,8,384]{2,1,0:T(8,128)(2,1)S(1)}, u32[]{:S(2)}, u32[]{:S(2)}) async-start(bf16[128,8,384]{2,1,0:T(8,128)(2,1)} %bitcast.18), calls=%async_computation.4 | async-start | bytes 1572864 | tf_op jit(solution)/shard_map/all_to_all | solution.py:682
  205.3 14.9 %collective-permute-start.41 = (bf16[32,4096]{1,0:T(8,128)(2,1)}, bf16[32,4096]{1,0:T(8,128)(2,1)S(1)}, u32[]{:S(2)}, u32[]{:S(2)}) collective-permute-start(bf16[32,4096]{1,0:T(8,128)(2,1)} %get-tuple-element.272), channel_id=1, source_target_pairs={{0,16},{16,0},{1,17},{17,1},{2,18},{18,2},{3,19},{19,3},{4,20},{20... | collective-permute-start | bytes 786440 | tf_op jit(solution)/shard_map/ppermute | solution.py:22
  206.0 14.9 %collective-permute-start.40 = (bf16[32,4096]{1,0:T(8,128)(2,1)}, bf16[32,4096]{1,0:T(8,128)(2,1)}, u32[]{:S(2)}, u32[]{:S(2)}) collective-permute-start(bf16[32,4096]{1,0:T(8,128)(2,1)} %get-tuple-element.270), channel_id=1, source_target_pairs={{0,2},{2,0},{1,3},{3,1},{4,6},{6,4},{5,7},{7,5},{8,10},{10,8},{9,1... | collective-permute-start | bytes 786440 | tf_op jit(solution)/shard_map/ppermute | solution.py:22
  213.3 35.8 %all-to-all-start.5 = ((bf16[64,32,512]{2,1,0:T(8,128)(2,1)}), bf16[64,32,512]{2,1,0:T(8,128)(2,1)S(1)}, u32[]{:S(2)}, u32[]{:S(2)}) async-start(bf16[64,32,512]{2,1,0:T(8,128)(2,1)} %shard_map.147), calls=%async_computation.5 | async-start | bytes 4194304 | tf_op jit(solution)/shard_map/all_to_all | solution.py:707
  224.2 14.6 %collective-permute-start.49 = (f32[4,4,256]{2,1,0:T(4,128)S(1)}, f32[4,4,256]{2,1,0:T(4,128)S(1)}, u32[]{:S(2)}, u32[]{:S(2)}) collective-permute-start(f32[4,4,256]{2,1,0:T(4,128)S(1)} %get-tuple-element.295), channel_id=1, source_target_pairs={{0,8},{4,12},{8,0},{12,4},{1,9},{5,13},{9,1},{13,5},{2,10},{6,14},... | collective-permute-start | bytes 49160 | tf_op jit(solution)/shard_map/ppermute | solution.py:18
  226.9 12.0 %collective-permute-start.50 = (f32[4,4,256]{2,1,0:T(4,128)S(1)}, f32[4,4,256]{2,1,0:T(4,128)S(1)}, u32[]{:S(2)}, u32[]{:S(2)}) collective-permute-start(f32[4,4,256]{2,1,0:T(4,128)S(1)} %get-tuple-element.294), channel_id=1, source_target_pairs={{0,12},{4,0},{8,4},{12,8},{1,13},{5,1},{9,5},{13,9},{2,14},{6,2},{... | collective-permute-start | bytes 49160 | tf_op jit(solution)/shard_map/ppermute | solution.py:18
  (64 other events, 739.1 us)
